TPU v7x, 32 devices: a whole 2x2x4 slice. The times are simulated.
32 devices in a mesh: groups: 2 (over x), space: 16 (over z, y, core).
Axes of the slice: x: 2, y: 2, z: 4, core: 2. Of those that a mesh axis runs over, the one named last changes fastest.
Arguments:
- patterns: float32 [64, 2, 128, 512], P('groups', None, 'space'), parts along dimension 0, may hold values from -8 to 8
- cases: int32 [64], P('groups'), parts along dimension 0, may hold values from 0 to 31, each once
- density: float32 [256, 512], P(('groups', 'space')), parts along dimension 0, may hold values from 0.2 to 1
- supports: int32 [256, 512], P(('groups', 'space')), parts along dimension 0, may hold values 0 or 1
Outputs:
- sensitivity: float32 [256, 512], P(('groups', 'space')), parts along dimension 0
- compliance: float32 [64], P('groups'), parts along dimension 0
There are 2 independent parts, one for each index of `groups`. A program takes and returns all parts, laid end to end along the dimension named above; each array names one. Nothing has to cross between parts.
Inputs may be any that keep to these rules, and one draw needn't show every extreme that they name: `cases`: every pattern is used by exactly one case.
All inputs are finite; a program needn't handle non-finite values. No bound on the sum of `supports` on one device may be relied on, other than what follows from the above.
Results may differ from a plain program's by a relative error of at most 0.00015.
Values sent between devices are 32-bit elements; how exact they have to be, the bound alone decides.
No kernel may reach another device: no remote copies, remote signals or barrier semaphores. Data moves between devices by JAX's collectives and lax.ppermute only.
A program may use at most 64 MiB of HBM per device.

v0:
```python
import functools

import jax
import jax.numpy as jnp
from jax import lax
from jax.experimental import pallas as pl
from jax.experimental.pallas import tpu as pltpu
from jax.sharding import PartitionSpec as P

ITERS = 4
EMIN = 0.001
KAPPA = 1.0
NU = 0.3
CENTRE = 1.5
EDGE = 0.5
CORNER = 1.5 - 2.0**0.5

LO = ITERS
HI = ITERS + 1
MOMENTS = 2 * ITERS

STRETCH = 1.0 / (4.0 * (1.0 - NU * NU))
SHEAR = 1.0 / (8.0 * (1.0 + NU))
TWIST = (3.0 - NU) / (24.0 * (1.0 - NU * NU))

LANES = 128
SUB = 8
CHUNKS = 1


def from_next(x, lane):
    r = [pltpu.roll(p, LANES - 1, 1) for p in x]
    r.append(jnp.zeros_like(r[0]))
    return [jnp.where(lane == LANES - 1, r[c + 1], r[c]) for c in range(len(x))]


def from_prev(x, lane):
    r = [pltpu.roll(p, 1, 1) for p in x]
    r = [jnp.zeros_like(r[0])] + r
    return [jnp.where(lane == 0, r[c], r[c + 1]) for c in range(len(x))]


def pieces(row):
    return [row[..., c : c + LANES] for c in range(0, row.shape[-1], LANES)]


def mapped(f, *args):
    return [f(*a) for a in zip(*args)]


def pair_modes(x, lane):
    n = from_next(x, lane)
    return mapped(lambda a, b: a + b, x, n), mapped(lambda a, b: b - a, x, n)


def element_modes(here, above):
    (p0, m0), (p1, m1) = here, above
    gx = mapped(lambda a, b: b - a, p0, p1)
    gy = mapped(lambda a, b: b + a, m0, m1)
    tw = mapped(lambda a, b: b - a, m0, m1)
    return gx, gy, tw


def krylov_kernel(
    groups, own, lo, hi, dens, sup, *rest
):
    if len(rest) == 9:
        before, rest = rest[0], rest[1:]
    else:
        before = None
    v, msg, dext, ea, ec, eh, free, acc = rest
    rows, cols = dens.shape
    total_rows = rows + LO + HI
    lane = lax.broadcasted_iota(jnp.int32, (SUB, LANES), 1)
    sublane = lax.broadcasted_iota(jnp.int32, (SUB, LANES), 0)
    part = groups * SUB
    lo_base = part * 2 * LO
    hi_base = part * 2 * HI

    for r in range(total_rows):
        if r < LO:
            d = lo[lo_base + r : lo_base + r + 1, :]
            f = lo[lo_base + LO + r : lo_base + LO + r + 1, :]
        elif r < LO + rows:
            d = dens[r - LO : r - LO + 1, :]
            f = 1.0 - sup[r - LO : r - LO + 1, :].astype(jnp.float32)
        else:
            k = r - LO - rows
            d = hi[hi_base + k : hi_base + k + 1, :]
            f = hi[hi_base + HI + k : hi_base + HI + k + 1, :]
        free[r] = jnp.broadcast_to(f, (SUB, cols))
        dext[r : r + 1, :] = d
        if r < total_rows - 1:
            y = jnp.where(d > 0.0, EMIN + d * d * d * (1.0 - EMIN), 0.0)
            y = jnp.broadcast_to(y, (SUB, cols))
            ea[r] = y * STRETCH
            ec[r] = y * SHEAR
            eh[r] = y * TWIST

    def group(g, _):
        at = pl.ds(pl.multiple_of(g * SUB, SUB), SUB)
        for r in range(total_rows):
            for k in range(2):
                if r < LO:
                    x = lo[pl.ds(pl.multiple_of((k * LO + r) * part + g * SUB, SUB), SUB), :]
                elif r < LO + rows:
                    x = own[pl.ds(pl.multiple_of((k * rows + r - LO) * part + g * SUB, SUB), SUB), :]
                else:
                    x = hi[pl.ds(pl.multiple_of((k * HI + r - LO - rows) * part + g * SUB, SUB), SUB), :]
                v[0, k, r, at, :] = x * free[r]

        sums = [None] * MOMENTS

        def add(i, a, b):
            for p, q in zip(a, b):
                sums[i] = p * q if sums[i] is None else sums[i] + p * q

        for it in range(ITERS):
            last = it == ITERS - 1
            first_e = LO if last else it
            last_e = LO + rows - 1 if last else total_rows - 2 - it
            here = [pair_modes(pieces(v[it, k, first_e, at, :]), lane) for k in range(2)]
            prior = None
            for e in range(first_e, last_e + 1):
                above = [pair_modes(pieces(v[it, k, e + 1, at, :]), lane) for k in range(2)]
                gxu, gyu, twu = element_modes(here[0], above[0])
                gxv, gyv, twv = element_modes(here[1], above[1])
                here = above
                a, c, h = pieces(ea[e]), pieces(ec[e]), pieces(eh[e])
                tx = mapped(lambda y, s, t: y * (s + NU * t), a, gxu, gyv)
                ty = mapped(lambda y, s, t: y * (NU * s + t), a, gxu, gyv)
                gs = mapped(lambda s, t: s + t, gyu, gxv)
                tg = mapped(lambda y, s: y * s, c, gs)
                hu = mapped(lambda y, s: y * s, h, twu)
                hv = mapped(lambda y, s: y * s, h, twv)
                if last:
                    for s, t in ((tx, gxu), (ty, gyv), (tg, gs), (hu, twu), (hv, twv)):
                        add(MOMENTS - 1, s, t)
                    continue
                up = [
                    (tx, mapped(lambda s, t: s + t, tg, hu)),
                    (tg, mapped(lambda s, t: s + t, ty, hv)),
                ]
                if prior is not None:
                    dn = [mapped(lambda s, t: s - t, tg, hu), mapped(lambda s, t: s - t, ty, hv)]
                    mask = pieces(free[e])
                    for k in range(2):
                        t = mapped(lambda s, t: s - t, prior[k][0], up[k][0])
                        q = mapped(lambda s, t: s + t, prior[k][1], dn[k])
                        left = mapped(lambda s, t: s - t, t, q)
                        right = from_prev(mapped(lambda s, t: s + t, t, q), lane)
                        out = mapped(lambda s, t, m: (s + t) * m, left, right, mask)
                        for c0, o in enumerate(out):
                            v[it + 1, k, e, at, c0 * LANES : (c0 + 1) * LANES] = o
                        if LO <= e < LO + rows:
                            src = pieces(v[it, k, e, at, :])
                            if it == 0:
                                add(0, src, src)
                            add(2 * it + 1, src, out)
                            add(2 * it + 2, out, out)
                prior = up
        for i in range(MOMENTS):
            acc[i, at, :] = sums[i]
        return 0

    lax.fori_loop(0, groups, group, 0)

    for i in range(MOMENTS):
        row = jnp.zeros((SUB, LANES), jnp.float32)
        for g in range(groups):
            s = jnp.sum(acc[i, g * SUB : (g + 1) * SUB, :], axis=1, keepdims=True)
            row = row + jnp.where(lane == sublane + (g * SUB), s, 0.0)
        msg[i : i + 1, :] = jnp.sum(row, axis=0, keepdims=True)


def coefficients(m):
    zero = jnp.zeros_like(m[0])
    s_prev, s = [zero] * MOMENTS, list(m)
    a, b = [m[1] / m[0]], [m[0]]
    fine = [m[0] > 0.0]
    for k in range(1, ITERS):
        n = [None] * MOMENTS
        for l in range(k, MOMENTS - k):
            n[l] = s[l + 1] - a[k - 1] * s[l]
            if k > 1:
                n[l] = n[l] - b[k - 1] * s_prev[l]
        scale = jnp.abs(s[k + 1]) + jnp.abs(a[k - 1] * s[k])
        fine.append(fine[-1] & (n[k] > 1e-6 * scale))
        a.append(n[k + 1] / n[k] - s[k] / s[k - 1])
        b.append(n[k] / s[k - 1])
        s_prev, s = s, n
    x = [zero] * ITERS
    r = [jnp.ones_like(zero)] + [zero] * (ITERS - 1)
    p = list(r)
    total = zero
    rr, d, good = m[0], a[0], fine[0] & (a[0] > 0.0)
    for k in range(ITERS):
        alpha = jnp.where(good, 1.0 / d, 0.0)
        total = total + jnp.where(good, alpha * rr, 0.0)
        for j in range(k + 1):
            x[j] = x[j] + jnp.where(good, alpha * p[j], 0.0)
        if k + 1 < ITERS:
            r = [r[j] - (alpha * p[j - 1] if j else 0.0) for j in range(ITERS)]
            ratio = b[k + 1] / (d * d)
            p = [r[j] + ratio * p[j] for j in range(ITERS)]
            rr = rr * ratio
            d = a[k + 1] - b[k + 1] / d
            good = good & fine[k + 1] & (d > 0.0)
    return x, total


def finish_kernel(count, elements, *refs):
    vs = refs[:CHUNKS]
    msgs, dext, cases, sens, comp, energy, rimmed = refs[CHUNKS:]
    rows, cols = sens.shape
    lane = lax.broadcasted_iota(jnp.int32, (SUB, LANES), 1)
    sublane = lax.broadcasted_iota(jnp.int32, (SUB, LANES), 0)
    m = msgs[0]
    for i in range(1, msgs.shape[0]):
        m = m + msgs[i]
    xs, total = coefficients([m[i : i + 1, :] for i in range(MOMENTS)])
    real = lax.broadcasted_iota(jnp.int32, (1, LANES), 1) < count
    total = jnp.where(real, total, 0.0)
    mean = jnp.sum(total, axis=1, keepdims=True) / count
    weight = 1.0 / count + 2.0 * KAPPA / count * (total - mean) / mean

    def by_case(row, g):
        s = jnp.where(lane == sublane + g * SUB, jnp.broadcast_to(row, (SUB, LANES)), 0.0)
        return jnp.broadcast_to(jnp.sum(s, axis=1, keepdims=True), (SUB, LANES))

    picked = jnp.zeros((SUB, LANES), jnp.float32)
    for g in range(count // SUB):
        picked = picked + jnp.where(
            jnp.broadcast_to(cases[...], (SUB, LANES)) == sublane + g * SUB, by_case(total, g), 0.0
        )
    comp[...] = jnp.sum(picked, axis=0, keepdims=True) / elements

    span = rows + 2
    first = True
    for ref in vs:
        groups = ref.shape[3] // SUB
        for g in range(groups):
            gi = vs.index(ref) * groups + g
            at = slice(g * SUB, (g + 1) * SUB)
            co = [by_case(x, gi) for x in xs]
            w = by_case(weight, gi)

            def node(r):
                out = []
                for k in range(2):
                    vals = [pieces(ref[j, k, r, at, :]) for j in range(ITERS)]
                    x = mapped(lambda *q: sum(c * s for c, s in zip(co[1:], q[1:])) + co[0] * q[0], *vals)
                    out.append(pair_modes(x, lane))
                return out

            here = node(LO - 1)
            for e in range(span):
                above = node(LO + e)
                gxu, gyu, twu = element_modes(here[0], above[0])
                gxv, gyv, twv = element_modes(here[1], above[1])
                here = above
                for c in range(cols // LANES):
                    sh = gyu[c] + gxv[c]
                    en = STRETCH * (gxu[c] * gxu[c] + gyv[c] * gyv[c] + (2.0 * NU) * (gxu[c] * gyv[c]))
                    en = en + SHEAR * (sh * sh) + TWIST * (twu[c] * twu[c] + twv[c] * twv[c])
                    en = w * en
                    cs = slice(c * LANES, (c + 1) * LANES)
                    energy[e, :, cs] = en if first else energy[e, :, cs] + en
            first = False

    for e in range(span):
        d = dext[LO - 1 + e : LO + e, :]
        s = jnp.sum(energy[e], axis=0, keepdims=True)
        rimmed[e : e + 1, :] = (-(elements / mean[:, :1]) * 3.0 * (1.0 - EMIN)) * (d * d * d * s)

    def taps(get):
        up, mid, dn = get(0), get(1), get(2)
        side = mapped(lambda a, b: a + b, up, dn)
        total = mapped(lambda a, b: CENTRE * a + EDGE * b, mid, side)
        sides = mapped(lambda a, b: EDGE * a + CORNER * b, mid, side)
        left, right = from_prev(sides, lane), from_next(sides, lane)
        return mapped(lambda a, b, c: a + b + c, total, left, right)

    top = taps(lambda i: pieces(rimmed[i : i + rows, :]))
    one = taps(
        lambda i: pieces(jnp.where(dext[LO - 1 + i : LO - 1 + i + rows, :] > 0.0, 1.0, 0.0))
    )
    for c in range(cols // LANES):
        cs = slice(c * LANES, (c + 1) * LANES)
        sens[:, cs] = top[c] / (one[c] * dext[LO : LO + rows, cs])


def local(patterns, cases, density, supports):
    rows, cols = density.shape
    count = patterns.shape[0]
    tiles = lax.axis_size("space")
    part = count // CHUNKS
    groups = part // SUB
    total_rows = rows + LO + HI
    free = (1 - supports).astype(jnp.float32)
    up = [(i, i + 1) for i in range(tiles - 1)]
    down = [(i + 1, i) for i in range(tiles - 1)]

    def by_row(x):
        return jnp.transpose(x, (1, 2, 0, 3)).reshape(-1, cols)

    vmem = pl.BlockSpec(memory_space=pltpu.VMEM)

    lows, highs = [], []
    for c in range(CHUNKS):
        mine = patterns[c * part : (c + 1) * part]
        low = by_row(mine[:, :, rows - LO :])
        high = by_row(mine[:, :, :HI])
        low = jnp.concatenate([low, density[rows - LO :], free[rows - LO :]], 0)
        high = jnp.concatenate([high, density[:HI], free[:HI]], 0)
        lows.append(lax.ppermute(low, "space", up))
        highs.append(lax.ppermute(high, "space", down))

    vs = []
    for c in range(CHUNKS):
        v, msg, dext = pl.pallas_call(
            functools.partial(krylov_kernel, groups),
            out_shape=(
                jax.ShapeDtypeStruct((ITERS, 2, total_rows, part, cols), jnp.float32),
                jax.ShapeDtypeStruct((MOMENTS, LANES), jnp.float32),
                jax.ShapeDtypeStruct((total_rows, cols), jnp.float32),
            ),
            in_specs=[vmem] * 5,
            out_specs=(vmem,) * 3,
            scratch_shapes=[
                pltpu.VMEM((total_rows - 1, SUB, cols), jnp.float32),
                pltpu.VMEM((total_rows - 1, SUB, cols), jnp.float32),
                pltpu.VMEM((total_rows - 1, SUB, cols), jnp.float32),
                pltpu.VMEM((total_rows, SUB, cols), jnp.float32),
                pltpu.VMEM((MOMENTS, part, LANES), jnp.float32),
            ],
            compiler_params=pltpu.CompilerParams(vmem_limit_bytes=12 * 2**20),
            name="krylov",
        )(by_row(patterns[c * part : (c + 1) * part]), lows[c], highs[c], density, supports)
        vs.append(v)

    msgs = lax.all_to_all(jnp.broadcast_to(msg[None], (tiles,) + msg.shape), "space", 0, 0)
    padded = jnp.pad(cases, (0, LANES - count))[None]
    sens, comp = pl.pallas_call(
        functools.partial(finish_kernel, count, rows * tiles * cols),
        out_shape=(
            jax.ShapeDtypeStruct((rows, cols), jnp.float32),
            jax.ShapeDtypeStruct((1, LANES), jnp.float32),
        ),
        in_specs=[vmem] * (CHUNKS + 3),
        out_specs=(vmem,) * 2,
        scratch_shapes=[
            pltpu.VMEM((rows + 2, SUB, cols), jnp.float32),
            pltpu.VMEM((rows + SUB, cols), jnp.float32),
        ],
        compiler_params=pltpu.CompilerParams(vmem_limit_bytes=12 * 2**20),
        name="finish",
    )(*vs, msgs, dext, padded)
    return sens, comp[0, :count]


def solution(mesh):
    in_specs = (
        P("groups", None, "space", None),
        P("groups"),
        P(("groups", "space"), None),
        P(("groups", "space"), None),
    )
    out_specs = (P(("groups", "space"), None), P("groups"))
    return jax.shard_map(local, mesh=mesh, in_specs=in_specs, out_specs=out_specs, check_vma=False)
```

profile of v0, /device:TPU:0, one launch (start us, length us, event | category | flops | bytes accessed | tf_op | source)
XLA Modules:
  0.0 58.4 jit_solution(13214356635096061005)
XLA Ops:
  0.6 0.0 copy-start.3
  0.6 0.0 copy-start.4
  0.7 0.0 copy-start.2
  0.7 0.0 copy-start.5
  0.7 0.8 %subtract_convert_fusion = f32[8,512]{1,0:T(8,128)S(1)} fusion(s32[8,512]{1,0:T(8,128)} %sup.1), kind=kLoop, calls=%fused_computation.4 | loop fusion | flops 8192 | bytes 32768 | tf_op jit(solution)/shard_map/convert_element_type | solution.py:300
  1.5 1.3 %slice_bitcast_fusion = f32[2,5,32,512]{3,1,0,2:T(8,128)S(1)} fusion(f32[32,2,8,512]{3,2,1,0:T(8,128)} %param.4), kind=kLoop, calls=%fused_computation | loop fusion | bytes 1310720 | tf_op jit(solution)/shard_map/transpose | solution.py:305
  2.8 0.4 copy.8
  3.2 0.8 %pad_maximum_fusion = f32[330,512]{1,0:T(8,128)S(1)} fusion(f32[5,512]{1,0:T(8,128)S(1)} %bitcast.19, f32[5,512]{1,0:T(8,128)} %bitcast.15, f32[320,512]{1,0:T(8,128)S(1)} %bitcast.17), kind=kLoop, calls=%fused_computation.1 | loop fusion | flops 337920 | bytes 1351680 | tf_op jit(solution)/shard_map/concatenate | solution.py:315
  4.0 1.3 %collective-permute-start.1 = (f32[330,512]{1,0:T(8,128)S(1)}, f32[330,512]{1,0:T(8,128)S(1)}, u32[]{:S(2)}, u32[]{:S(2)}) collective-permute-start(f32[330,512]{1,0:T(8,128)S(1)} %pad_maximum_fusion), channel_id=1, source_target_pairs={{1,0},{2,1},{3,2},{4,3},{5,4},{6,5},{7,6},{8,7},{9,8},{10,9},{11,1... | collective-permute-start | bytes 2027528 | tf_op jit(solution)/shard_map/ppermute | solution.py:317
  5.3 1.4 %slice_bitcast_fusion.1 = f32[2,4,32,512]{3,1,0,2:T(4,128)S(1)} fusion(f32[32,2,8,512]{3,2,1,0:T(8,128)} %param.4), kind=kLoop, calls=%fused_computation.3 | loop fusion | bytes 1048576 | tf_op jit(solution)/shard_map/transpose | solution.py:305
  6.7 0.7 %slice.22 = f32[4,512]{1,0:T(4,128)S(1)} slice(f32[8,512]{1,0:T(8,128)} %dens.1), slice={[4:8], [0:512]} | slice | bytes 16384 | tf_op jit(solution)/shard_map/slice | solution.py:314
  7.4 0.3 copy.7
  7.7 3.1 %collective-permute-start = (f32[264,512]{1,0:T(8,128)S(1)}, f32[264,512]{1,0:T(8,128)S(1)}, u32[]{:S(2)}, u32[]{:S(2)}) collective-permute-start(f32[264,512]{1,0:T(8,128)S(1)} %pad_maximum_fusion.1), channel_id=1, source_target_pairs={{0,1},{1,2},{2,3},{3,4},{4,5},{5,6},{6,7},{7,8},{8,9},{9,10},{10,1... | collective-permute-start | bytes 1622024 | tf_op jit(solution)/shard_map/ppermute | solution.py:316
  10.8 0.0 copy-done.4
  10.8 0.6 %copy.6 = f32[2,8,32,512]{3,2,1,0:T(8,128)S(1)} copy(f32[2,8,32,512]{3,1,0,2:T(8,128)S(1)} %bitcast.16) | data formatting | bytes 2097152 | tf_op jit(solution)/shard_map/transpose | solution.py:305
  11.4 0.9 %collective-permute-done.lo = f32[264,512]{1,0:T(8,128)S(1)} collective-permute-done((f32[264,512]{1,0:T(8,128)S(1)}, f32[264,512]{1,0:T(8,128)S(1)}, u32[]{:S(2)}, u32[]{:S(2)}) %collective-permute-start) | collective-permute-done | bytes 540704 | tf_op jit(solution)/shard_map/ppermute | solution.py:316
  12.3 0.0 collective-permute-done.1.hi
  12.3 0.0 copy-done.3
  12.3 0.0 copy-done.2
  12.3 12.1 %krylov.1 = (f32[4,2,17,32,512]{4,3,2,1,0:T(8,128)S(1)}, f32[8,128]{1,0:T(8,128)S(1)}, f32[17,512]{1,0:T(8,128)S(1)}) custom-call(f32[512,512]{1,0:T(8,128)S(1)} %bitcast.14, f32[264,512]{1,0:T(8,128)S(1)} %collective-permute-done.lo, f32[330,512]{1,0:T(8,128)S(1)} %collective-permute-done.1.hi, f32[8,512]{1,0:T(8,128)S(1)} %copy-done.2, s32[8,512]{1,0:T(8,128)S(1)} %copy-done.3), custom_call_target="tpu_custom_call" | custom-call | tf_op jit(solution)/shard_map/krylov/pallas_call | solution.py:321
  24.5 0.0 copy-start
  24.5 3.4 %copy-done = f32[4,2,17,32,512]{4,3,2,1,0:T(8,128)} copy-done((f32[4,2,17,32,512]{4,3,2,1,0:T(8,128)}, f32[4,2,17,32,512]{4,3,2,1,0:T(8,128)S(1)}, u32[]{:S(2)}) %copy-start) | copy-done | bytes 8912920
  27.9 0.6 %broadcast_in_dim.4 = f32[16,8,128]{2,1,0:T(8,128)} broadcast(f32[8,128]{1,0:T(8,128)S(1)} %get-tuple-element.8), dimensions={1,2} | broadcast | bytes 69632 | tf_op jit(solution)/shard_map/broadcast_in_dim | solution.py:342
  28.5 17.0 %all-to-all-start = ((f32[16,8,128]{2,1,0:T(8,128)}), f32[16,8,128]{2,1,0:T(8,128)S(1)}, u32[]{:S(2)}, u32[]{:S(2)}) async-start(f32[16,8,128]{2,1,0:T(8,128)} %broadcast_in_dim.4), calls=%async_computation | async-start | bytes 131072 | tf_op jit(solution)/shard_map/all_to_all | solution.py:342
  45.5 0.0 copy-done.5
  45.5 6.9 %all-to-all-done.refs_1_ = f32[16,8,128]{2,1,0:T(8,128)S(1)} async-done(((f32[16,8,128]{2,1,0:T(8,128)}), f32[16,8,128]{2,1,0:T(8,128)S(1)}, u32[]{:S(2)}, u32[]{:S(2)}) %all-to-all-start) | async-done | bytes 65568 | tf_op jit(solution)/shard_map/all_to_all | solution.py:342
  52.4 0.0 copy-start.1
  52.4 3.5 %copy-done.1 = f32[4,2,17,32,512]{4,3,2,1,0:T(8,128)S(1)} copy-done((f32[4,2,17,32,512]{4,3,2,1,0:T(8,128)S(1)}, f32[4,2,17,32,512]{4,3,2,1,0:T(8,128)}, u32[]{:S(2)}) %copy-start.1) | copy-done | bytes 8912920
  55.9 1.9 %finish.1 = (f32[8,512]{1,0:T(8,128)}, f32[1,128]{1,0:T(1,128)S(1)}) custom-call(f32[4,2,17,32,512]{4,3,2,1,0:T(8,128)S(1)} %copy-done.1, f32[16,8,128]{2,1,0:T(8,128)S(1)} %all-to-all-done.refs_1_, f32[17,512]{1,0:T(8,128)S(1)} %get-tuple-element.9.refs_2_, s32[1,128]{1,0:T(1,128)S(1)} %pad_bitcast_fusion.refs_3_), custom_call_target="tpu_custom_call" | custom-call | tf_op jit(solution)/shard_map/finish/pallas_call | solution.py:344
  57.9 0.5 slice_bitcast_fusion.2
  (3 shorter events, 0.0 us)
Async XLA Ops:
  0.6 11.7 %copy-start.3 = (s32[8,512]{1,0:T(8,128)S(1)}, s32[8,512]{1,0:T(8,128)}, u32[]{:S(2)}) copy-start(s32[8,512]{1,0:T(8,128)} %sup.1) | copy-start | bytes 49156
  0.6 10.2 %copy-start.4 = (f32[32,2,8,512]{3,2,1,0:T(8,128)S(1)}, f32[32,2,8,512]{3,2,1,0:T(8,128)}, u32[]{:S(2)}) copy-start(f32[32,2,8,512]{3,2,1,0:T(8,128)} %param.4) | copy-start | bytes 3145732
  0.7 11.7 %copy-start.2 = (f32[8,512]{1,0:T(8,128)S(1)}, f32[8,512]{1,0:T(8,128)}, u32[]{:S(2)}) copy-start(f32[8,512]{1,0:T(8,128)} %dens.1) | copy-start | bytes 49156
  0.7 44.8 %copy-start.5 = (s32[32]{0:T(128)S(1)}, s32[32]{0:T(128)}, u32[]{:S(2)}) copy-start(s32[32]{0:T(128)} %param.5) | copy-start | bytes 388
  4.0 8.4 %collective-permute-start.1 = (f32[330,512]{1,0:T(8,128)S(1)}, f32[330,512]{1,0:T(8,128)S(1)}, u32[]{:S(2)}, u32[]{:S(2)}) collective-permute-start(f32[330,512]{1,0:T(8,128)S(1)} %pad_maximum_fusion), channel_id=1, source_target_pairs={{1,0},{2,1},{3,2},{4,3},{5,4},{6,5},{7,6},{8,7},{9,8},{10,9},{11,1... | collective-permute-start | bytes 2027528 | tf_op jit(solution)/shard_map/ppermute | solution.py:317
  7.7 4.6 %collective-permute-start = (f32[264,512]{1,0:T(8,128)S(1)}, f32[264,512]{1,0:T(8,128)S(1)}, u32[]{:S(2)}, u32[]{:S(2)}) collective-permute-start(f32[264,512]{1,0:T(8,128)S(1)} %pad_maximum_fusion.1), channel_id=1, source_target_pairs={{0,1},{1,2},{2,3},{3,4},{4,5},{5,6},{6,7},{7,8},{8,9},{9,10},{10,1... | collective-permute-start | bytes 1622024 | tf_op jit(solution)/shard_map/ppermute | solution.py:316
  24.5 3.4 %copy-start = (f32[4,2,17,32,512]{4,3,2,1,0:T(8,128)}, f32[4,2,17,32,512]{4,3,2,1,0:T(8,128)S(1)}, u32[]{:S(2)}) copy-start(f32[4,2,17,32,512]{4,3,2,1,0:T(8,128)S(1)} %get-tuple-element.7.refs_0_) | copy-start | bytes 26738692
  28.5 23.9 %all-to-all-start = ((f32[16,8,128]{2,1,0:T(8,128)}), f32[16,8,128]{2,1,0:T(8,128)S(1)}, u32[]{:S(2)}, u32[]{:S(2)}) async-start(f32[16,8,128]{2,1,0:T(8,128)} %broadcast_in_dim.4), calls=%async_computation | async-start | bytes 131072 | tf_op jit(solution)/shard_map/all_to_all | solution.py:342
  52.4 3.5 %copy-start.1 = (f32[4,2,17,32,512]{4,3,2,1,0:T(8,128)S(1)}, f32[4,2,17,32,512]{4,3,2,1,0:T(8,128)}, u32[]{:S(2)}) copy-start(f32[4,2,17,32,512]{4,3,2,1,0:T(8,128)} %copy-done) | copy-start | bytes 26738692
where the time goes:
time: 58.9 us; the launch traced here: 58.4 us
  starting transfers between devices  21.3 us (36%)
  Pallas kernels  14.1 us (24%)
  local copies, waits for them, and re-layouts  12.8 us (22%)
  waiting for transfers between devices  7.76 us (13%)
  other arithmetic  1.61 us (3%)
  between operations  0.78 us (1%)
    all_to_all x1, starting transfers between devices, local(): lax.all_to_all(jnp.broadcast_to(msg[None], (tiles,) + msg.shape), 'space'...  17 us
    pallas_call x1, Pallas kernels, local(): pl.pallas_call(functools.partial(krylov_kernel, groups), out_shape=(jax.S...  12.1 us
    unnamed x12, local copies, waits for them, and re-layouts  6.98 us
    all_to_all x1, waiting for transfers between devices, local(): lax.all_to_all(jnp.broadcast_to(msg[None], (tiles,) + msg.shape), 'space'...  6.87 us
    transpose x5, local copies, waits for them, and re-layouts, by_row(): return jnp.transpose(x, (1, 2, 0, 3)).reshape(-1, cols)  3.98 us
    ppermute x1, starting transfers between devices, local(): lows.append(lax.ppermute(low, 'space', up))  3.06 us
    pallas_call x1, Pallas kernels, local(): pl.pallas_call(functools.partial(finish_kernel, count, rows * tiles * col...  1.94 us
    ppermute x1, starting transfers between devices, local(): highs.append(lax.ppermute(high, 'space', down))  1.29 us
  transfers between devices with their start and end apart: 3, of which 2 were waited for; matrix products, arithmetic and copies ran while one was open for 5% of the time, Pallas kernels for 0%

commit v1 on v0

--- a/solution.py
+++ b/solution.py
@@ -29,15 +29,22 @@
 
 
 def from_next(x, lane):
-    r = [pltpu.roll(p, LANES - 1, 1) for p in x]
-    r.append(jnp.zeros_like(r[0]))
-    return [jnp.where(lane == LANES - 1, r[c + 1], r[c]) for c in range(len(x))]
+    r = pltpu.roll(x[0], LANES - 1, 1)
+    return x[1:] + [jnp.where(lane == LANES - 1, 0.0, r)]
 
 
 def from_prev(x, lane):
-    r = [pltpu.roll(p, 1, 1) for p in x]
-    r = [jnp.zeros_like(r[0])] + r
-    return [jnp.where(lane == 0, r[c], r[c + 1]) for c in range(len(x))]
+    r = pltpu.roll(x[-1], 1, 1)
+    return [jnp.where(lane == 0, 0.0, r)] + x[:-1]
+
+
+def rearranged(x, perm):
+    high = x.astype(jnp.bfloat16)
+    rest = x - high.astype(jnp.float32)
+    mid = rest.astype(jnp.bfloat16)
+    low = (rest - mid.astype(jnp.float32)).astype(jnp.bfloat16)
+    a, b, c = [jnp.dot(t, perm, preferred_element_type=jnp.float32) for t in (high, mid, low)]
+    return (a + b) + c
 
 
 def pieces(row):
@@ -61,33 +68,69 @@
     return gx, gy, tw
 
 
-def krylov_kernel(
-    groups, own, lo, hi, dens, sup, *rest
-):
-    if len(rest) == 9:
+def pack_kernel(part, chunk, pat, dens, sup, own, lo, hi, perm, tmp):
+    rows, cols = dens.shape
+    width = cols // LANES
+    j = lax.broadcasted_iota(jnp.int32, (cols, LANES), 0)
+    l = lax.broadcasted_iota(jnp.int32, (cols, LANES), 1)
+    for c in range(width):
+        one = jnp.where(j == width * l + c, 1.0, 0.0).astype(jnp.bfloat16)
+        perm[:, c * LANES : (c + 1) * LANES] = one
+    start, size = chunk * part * 2 * rows, part * 2 * rows
+    for b in range(0, size, LANES):
+        y = rearranged(pat[start + b : start + b + LANES, :], perm[...])
+        for c, p in enumerate(pieces(y)):
+            tmp[c, b : b + LANES, :] = p
+    for k in range(2):
+        for r in range(rows):
+            for g in range(part // SUB):
+                for c in range(width):
+                    x = tmp[c, pl.ds((g * SUB * 2 + k) * rows + r, SUB, stride=2 * rows), :]
+                    cs = slice(c * LANES, (c + 1) * LANES)
+                    at = (k * rows + r) * part + g * SUB
+                    own[at : at + SUB, cs] = x
+                    if r >= rows - LO:
+                        at = (k * LO + r - rows + LO) * part + g * SUB
+                        lo[at : at + SUB, cs] = x
+                    if r < HI:
+                        at = (k * HI + r) * part + g * SUB
+                        hi[at : at + SUB, cs] = x
+    if chunk == 0:
+        both = jnp.concatenate([dens[...], 1.0 - sup[...].astype(jnp.float32)], 0)
+        both = rearranged(both, perm[...])
+        for i in range(2):
+            field = both[i * rows : (i + 1) * rows]
+            at = part * 2 * rows + i * rows
+            own[at : at + rows, :] = field
+            at = part * 2 * LO + i * LO
+            lo[at : at + LO, :] = field[rows - LO :]
+            at = part * 2 * HI + i * HI
+            hi[at : at + HI, :] = field[:HI]
+
+
+def krylov_kernel(groups, rows, chunk, own, lo, hi, own0, lo0, hi0, *rest):
+    if chunk:
         before, rest = rest[0], rest[1:]
-    else:
-        before = None
     v, msg, dext, ea, ec, eh, free, acc = rest
-    rows, cols = dens.shape
+    cols = own.shape[1]
     total_rows = rows + LO + HI
     lane = lax.broadcasted_iota(jnp.int32, (SUB, LANES), 1)
     sublane = lax.broadcasted_iota(jnp.int32, (SUB, LANES), 0)
     part = groups * SUB
-    lo_base = part * 2 * LO
-    hi_base = part * 2 * HI
+    lo_base, own_base, hi_base = part * 2 * LO, part * 2 * rows, part * 2 * HI
 
     for r in range(total_rows):
         if r < LO:
-            d = lo[lo_base + r : lo_base + r + 1, :]
-            f = lo[lo_base + LO + r : lo_base + LO + r + 1, :]
+            d = lo0[lo_base + r : lo_base + r + 1, :]
+            f = lo0[lo_base + LO + r : lo_base + LO + r + 1, :]
         elif r < LO + rows:
-            d = dens[r - LO : r - LO + 1, :]
-            f = 1.0 - sup[r - LO : r - LO + 1, :].astype(jnp.float32)
+            k = own_base + r - LO
+            d = own0[k : k + 1, :]
+            f = own0[k + rows : k + rows + 1, :]
         else:
             k = r - LO - rows
-            d = hi[hi_base + k : hi_base + k + 1, :]
-            f = hi[hi_base + HI + k : hi_base + HI + k + 1, :]
+            d = hi0[hi_base + k : hi_base + k + 1, :]
+            f = hi0[hi_base + HI + k : hi_base + HI + k + 1, :]
         free[r] = jnp.broadcast_to(f, (SUB, cols))
         dext[r : r + 1, :] = d
         if r < total_rows - 1:
@@ -169,8 +212,9 @@
         row = jnp.zeros((SUB, LANES), jnp.float32)
         for g in range(groups):
             s = jnp.sum(acc[i, g * SUB : (g + 1) * SUB, :], axis=1, keepdims=True)
-            row = row + jnp.where(lane == sublane + (g * SUB), s, 0.0)
-        msg[i : i + 1, :] = jnp.sum(row, axis=0, keepdims=True)
+            row = row + jnp.where(lane == sublane + (chunk * part + g * SUB), s, 0.0)
+        row = jnp.sum(row, axis=0, keepdims=True)
+        msg[i : i + 1, :] = row + before[i : i + 1, :] if chunk else row
 
 
 def coefficients(m):
@@ -211,7 +255,7 @@
 
 def finish_kernel(count, elements, *refs):
     vs = refs[:CHUNKS]
-    msgs, dext, cases, sens, comp, energy, rimmed = refs[CHUNKS:]
+    msgs, dext, cases, sens, comp, energy, rimmed, perm = refs[CHUNKS:]
     rows, cols = sens.shape
     lane = lax.broadcasted_iota(jnp.int32, (SUB, LANES), 1)
     sublane = lax.broadcasted_iota(jnp.int32, (SUB, LANES), 0)
@@ -228,11 +272,10 @@
         s = jnp.where(lane == sublane + g * SUB, jnp.broadcast_to(row, (SUB, LANES)), 0.0)
         return jnp.broadcast_to(jnp.sum(s, axis=1, keepdims=True), (SUB, LANES))
 
-    picked = jnp.zeros((SUB, LANES), jnp.float32)
+    picked = jnp.zeros((SUB, count), jnp.float32)
     for g in range(count // SUB):
-        picked = picked + jnp.where(
-            jnp.broadcast_to(cases[...], (SUB, LANES)) == sublane + g * SUB, by_case(total, g), 0.0
-        )
+        match = jnp.broadcast_to(cases[...], (SUB, count)) == sublane[:, :count] + g * SUB
+        picked = picked + jnp.where(match, by_case(total, g)[:, :count], 0.0)
     comp[...] = jnp.sum(picked, axis=0, keepdims=True) / elements
 
     span = rows + 2
@@ -281,13 +324,20 @@
         left, right = from_prev(sides, lane), from_next(sides, lane)
         return mapped(lambda a, b, c: a + b + c, total, left, right)
 
+    width = cols // LANES
+    i = lax.broadcasted_iota(jnp.int32, (LANES, cols), 0)
+    j = lax.broadcasted_iota(jnp.int32, (LANES, cols), 1)
+    for c in range(width):
+        one = jnp.where(j == width * i + c, 1.0, 0.0).astype(jnp.bfloat16)
+        perm[c * LANES : (c + 1) * LANES, :] = one
+
     top = taps(lambda i: pieces(rimmed[i : i + rows, :]))
     one = taps(
         lambda i: pieces(jnp.where(dext[LO - 1 + i : LO - 1 + i + rows, :] > 0.0, 1.0, 0.0))
     )
-    for c in range(cols // LANES):
-        cs = slice(c * LANES, (c + 1) * LANES)
-        sens[:, cs] = top[c] / (one[c] * dext[LO : LO + rows, cs])
+    own = pieces(dext[LO : LO + rows, :])
+    out = jnp.concatenate([t / (o * d) for t, o, d in zip(top, one, own)], 1)
+    sens[...] = rearranged(out, perm[...])
 
 
 def local(patterns, cases, density, supports):
@@ -297,35 +347,45 @@
     part = count // CHUNKS
     groups = part // SUB
     total_rows = rows + LO + HI
-    free = (1 - supports).astype(jnp.float32)
     up = [(i, i + 1) for i in range(tiles - 1)]
     down = [(i + 1, i) for i in range(tiles - 1)]
-
-    def by_row(x):
-        return jnp.transpose(x, (1, 2, 0, 3)).reshape(-1, cols)
-
+    flat = patterns.reshape(count * 2 * rows, cols)
     vmem = pl.BlockSpec(memory_space=pltpu.VMEM)
-
-    lows, highs = [], []
+    params = pltpu.CompilerParams(vmem_limit_bytes=12 * 2**20)
+
+    def shape(*dims):
+        return jax.ShapeDtypeStruct(dims, jnp.float32)
+
+    owns, lows, highs = [], [], []
     for c in range(CHUNKS):
-        mine = patterns[c * part : (c + 1) * part]
-        low = by_row(mine[:, :, rows - LO :])
-        high = by_row(mine[:, :, :HI])
-        low = jnp.concatenate([low, density[rows - LO :], free[rows - LO :]], 0)
-        high = jnp.concatenate([high, density[:HI], free[:HI]], 0)
+        extra = 0 if c else 2
+        own, low, high = pl.pallas_call(
+            functools.partial(pack_kernel, part, c),
+            out_shape=tuple(shape(n * (2 * part + extra), cols) for n in (rows, LO, HI)),
+            in_specs=[vmem] * 3,
+            out_specs=(vmem,) * 3,
+            scratch_shapes=[
+                pltpu.VMEM((cols, cols), jnp.bfloat16),
+                pltpu.VMEM((cols // LANES, part * 2 * rows, LANES), jnp.float32),
+            ],
+            compiler_params=params,
+            name="pack",
+        )(flat, density, supports)
+        owns.append(own)
         lows.append(lax.ppermute(low, "space", up))
         highs.append(lax.ppermute(high, "space", down))
 
-    vs = []
+    vs, msg = [], None
     for c in range(CHUNKS):
+        args = (owns[c], lows[c], highs[c], owns[0], lows[0], highs[0]) + ((msg,) if c else ())
         v, msg, dext = pl.pallas_call(
-            functools.partial(krylov_kernel, groups),
+            functools.partial(krylov_kernel, groups, rows, c),
             out_shape=(
-                jax.ShapeDtypeStruct((ITERS, 2, total_rows, part, cols), jnp.float32),
-                jax.ShapeDtypeStruct((MOMENTS, LANES), jnp.float32),
-                jax.ShapeDtypeStruct((total_rows, cols), jnp.float32),
+                shape(ITERS, 2, total_rows, part, cols),
+                shape(MOMENTS, LANES),
+                shape(total_rows, cols),
             ),
-            in_specs=[vmem] * 5,
+            in_specs=[vmem] * len(args),
             out_specs=(vmem,) * 3,
             scratch_shapes=[
                 pltpu.VMEM((total_rows - 1, SUB, cols), jnp.float32),
@@ -334,29 +394,30 @@
                 pltpu.VMEM((total_rows, SUB, cols), jnp.float32),
                 pltpu.VMEM((MOMENTS, part, LANES), jnp.float32),
             ],
-            compiler_params=pltpu.CompilerParams(vmem_limit_bytes=12 * 2**20),
+            compiler_params=params,
             name="krylov",
-        )(by_row(patterns[c * part : (c + 1) * part]), lows[c], highs[c], density, supports)
+        )(*args)
         vs.append(v)
 
-    msgs = lax.all_to_all(jnp.broadcast_to(msg[None], (tiles,) + msg.shape), "space", 0, 0)
-    padded = jnp.pad(cases, (0, LANES - count))[None]
+    b = 1
+    while b < tiles:
+        msg = msg + lax.ppermute(msg, "space", [(i, i ^ b) for i in range(tiles)])
+        b *= 2
+    msgs = msg[None]
     sens, comp = pl.pallas_call(
         functools.partial(finish_kernel, count, rows * tiles * cols),
-        out_shape=(
-            jax.ShapeDtypeStruct((rows, cols), jnp.float32),
-            jax.ShapeDtypeStruct((1, LANES), jnp.float32),
-        ),
+        out_shape=(shape(rows, cols), shape(1, count)),
         in_specs=[vmem] * (CHUNKS + 3),
         out_specs=(vmem,) * 2,
         scratch_shapes=[
             pltpu.VMEM((rows + 2, SUB, cols), jnp.float32),
             pltpu.VMEM((rows + SUB, cols), jnp.float32),
+            pltpu.VMEM((cols, cols), jnp.bfloat16),
         ],
-        compiler_params=pltpu.CompilerParams(vmem_limit_bytes=12 * 2**20),
+        compiler_params=params,
         name="finish",
-    )(*vs, msgs, dext, padded)
-    return sens, comp[0, :count]
+    )(*vs, msgs, dext, cases[None])
+    return sens, comp.reshape(count)
 
 
 def solution(mesh):

time: 58.9 us -> 46.6 us (0.79)
  local copies, waits for them, and re-layouts: 12.8 us -> 3.31 us
  Pallas kernels: 14.1 us -> 9.37 us
  starting transfers between devices: 21.3 us -> 25 us
  other arithmetic: 1.61 us -> 0.01 us
    ppermute x0 -> x4, starting transfers between devices: none -> 20.6 us  [local(): msg = msg + lax.ppermute(msg, 'space', [(i, i ^ b) for i in range(tiles)])]
    all_to_all x1 -> x0, starting transfers between devices: 17 us -> none  [local(): lax.all_to_all(jnp.broadcast_to(msg[None], (tiles,) + msg.shape), 'space'...]
    all_to_all x1 -> x0, waiting for transfers between devices: 6.87 us -> none  [local(): lax.all_to_all(jnp.broadcast_to(msg[None], (tiles,) + msg.shape), 'space'...]
    ppermute x0 -> x4, waiting for transfers between devices: none -> 6.35 us  [local(): msg = msg + lax.ppermute(msg, 'space', [(i, i ^ b) for i in range(tiles)])]
    pallas_call x1 -> x2, Pallas kernels: 12.1 us -> 7.18 us  [the longest x1 5.58 us: local(): pl.pallas_call(functools.partial(krylov_kernel, groups, rows, c), out_sha...]
    transpose x5 -> x0, local copies, waits for them, and re-layouts: 3.98 us -> none  [by_row(): return jnp.transpose(x, (1, 2, 0, 3)).reshape(-1, cols)]
    unnamed x12 -> x8, local copies, waits for them, and re-layouts: 6.98 us -> 3.31 us
    concatenate x2 -> x0, other arithmetic: 0.81 us -> none  [the longest x1 0.77 us: local(): high = jnp.concatenate([high, density[:HI], free[:HI]], 0)]
  transfers between devices with their start and end apart: 3 -> 6, of which waited for: 2 -> 5; matrix products, arithmetic and copies ran while one was open for 5% -> 0% of each run, Pallas kernels for 0% -> 0%
where the time goes in v1:
time: 46.6 us; the launch traced here: 46.2 us
  starting transfers between devices  25 us (54%)
  Pallas kernels  9.37 us (20%)
  waiting for transfers between devices  7.86 us (17%)
  local copies, waits for them, and re-layouts  3.31 us (7%)
  between operations  0.67 us (1%)
    ppermute x4, starting transfers between devices, local(): msg = msg + lax.ppermute(msg, 'space', [(i, i ^ b) for i in range(tiles)])  20.6 us
    ppermute x4, waiting for transfers between devices, local(): msg = msg + lax.ppermute(msg, 'space', [(i, i ^ b) for i in range(tiles)])  6.35 us
    pallas_call x1, Pallas kernels, local(): pl.pallas_call(functools.partial(krylov_kernel, groups, rows, c), out_sha...  5.58 us
    unnamed x8, local copies, waits for them, and re-layouts  3.31 us
    ppermute x1, starting transfers between devices, local(): lows.append(lax.ppermute(low, 'space', up))  3.06 us
    pallas_call x1, Pallas kernels, local(): pl.pallas_call(functools.partial(finish_kernel, count, rows * tiles * col...  2.18 us
    pallas_call x1, Pallas kernels, local(): pl.pallas_call(functools.partial(pack_kernel, part, c), out_shape=tuple((...  1.6 us
    ppermute x1, waiting for transfers between devices, local(): lows.append(lax.ppermute(low, 'space', up))  1.51 us
  transfers between devices with their start and end apart: 6, of which 5 were waited for; matrix products, arithmetic and copies ran while one was open for 0% of the time, Pallas kernels for 0%

profile of v1, /device:TPU:0, one launch (start us, length us, event | category | flops | bytes accessed | tf_op | source)
XLA Modules:
  0.0 46.2 jit_solution(3291184749017179557)
XLA Ops:
  0.6 0.0 copy-start
  0.6 1.2 %copy-done = f32[32,2,8,512]{3,2,1,0:T(8,128)S(1)} copy-done((f32[32,2,8,512]{3,2,1,0:T(8,128)S(1)}, f32[32,2,8,512]{3,2,1,0:T(8,128)}, u32[]{:S(2)}) %copy-start) | copy-done | bytes 1048600
  1.9 0.0 copy-start.1
  1.9 0.7 %copy-done.1 = f32[8,512]{1,0:T(8,128)S(1)} copy-done((f32[8,512]{1,0:T(8,128)S(1)}, f32[8,512]{1,0:T(8,128)}, u32[]{:S(2)}) %copy-start.1) | copy-done | bytes 16408
  2.6 0.0 copy-start.2
  2.6 0.7 %copy-done.2 = s32[8,512]{1,0:T(8,128)S(1)} copy-done((s32[8,512]{1,0:T(8,128)S(1)}, s32[8,512]{1,0:T(8,128)}, u32[]{:S(2)}) %copy-start.2) | copy-done | bytes 16408
  3.3 1.6 %pack.1 = (f32[528,512]{1,0:T(8,128)S(1)}, f32[264,512]{1,0:T(8,128)S(1)}, f32[330,512]{1,0:T(8,128)S(1)}) custom-call(f32[512,512]{1,0:T(8,128)S(1)} %bitcast.5, f32[8,512]{1,0:T(8,128)S(1)} %copy-done.1, s32[8,512]{1,0:T(8,128)S(1)} %copy-done.2), custom_call_target="tpu_custom_call" | custom-call | tf_op jit(solution)/shard_map/pack/pallas_call | solution.py:362
  4.9 1.3 %collective-permute-start.1 = (f32[330,512]{1,0:T(8,128)S(1)}, f32[330,512]{1,0:T(8,128)S(1)}, u32[]{:S(2)}, u32[]{:S(2)}) collective-permute-start(f32[330,512]{1,0:T(8,128)S(1)} %get-tuple-element.12), channel_id=1, source_target_pairs={{1,0},{2,1},{3,2},{4,3},{5,4},{6,5},{7,6},{8,7},{9,8},{10,9},{11,1... | collective-permute-start | bytes 2027528 | tf_op jit(solution)/shard_map/ppermute | solution.py:376
  6.2 3.1 %collective-permute-start = (f32[264,512]{1,0:T(8,128)S(1)}, f32[264,512]{1,0:T(8,128)S(1)}, u32[]{:S(2)}, u32[]{:S(2)}) collective-permute-start(f32[264,512]{1,0:T(8,128)S(1)} %get-tuple-element.11), channel_id=1, source_target_pairs={{0,1},{1,2},{2,3},{3,4},{4,5},{5,6},{6,7},{7,8},{8,9},{9,10},{10,1... | collective-permute-start | bytes 1622024 | tf_op jit(solution)/shard_map/ppermute | solution.py:375
  9.3 1.5 %collective-permute-done.lo.lo0 = f32[264,512]{1,0:T(8,128)S(1)} collective-permute-done((f32[264,512]{1,0:T(8,128)S(1)}, f32[264,512]{1,0:T(8,128)S(1)}, u32[]{:S(2)}, u32[]{:S(2)}) %collective-permute-start) | collective-permute-done | bytes 540704 | tf_op jit(solution)/shard_map/ppermute | solution.py:375
  10.8 0.0 collective-permute-done.1.hi.hi0
  10.8 5.6 %krylov.1 = (f32[4,2,17,32,512]{4,3,2,1,0:T(8,128)S(1)}, f32[8,128]{1,0:T(8,128)S(1)}, f32[17,512]{1,0:T(8,128)S(1)}) custom-call(f32[528,512]{1,0:T(8,128)S(1)} %get-tuple-element.10.own.own0, f32[264,512]{1,0:T(8,128)S(1)} %collective-permute-done.lo.lo0, f32[330,512]{1,0:T(8,128)S(1)} %collective-permute-done.1.hi.hi0, ...), custom_call_target="tpu_custom_call" | custom-call | tf_op jit(solution)/shard_map/krylov/pallas_call | solution.py:381
  16.4 13.7 %collective-permute-start.2 = (f32[8,128]{1,0:T(8,128)S(1)}, f32[8,128]{1,0:T(8,128)S(1)}, u32[]{:S(2)}, u32[]{:S(2)}) collective-permute-start(f32[8,128]{1,0:T(8,128)S(1)} %get-tuple-element.14), channel_id=1, source_target_pairs={{0,1},{1,0},{2,3},{3,2},{4,5},{5,4},{6,7},{7,6},{8,9},{9,8},{10,11... | collective-permute-start | bytes 12296 | tf_op jit(solution)/shard_map/ppermute | solution.py:404
  30.1 0.8 %collective-permute-done.2 = f32[8,128]{1,0:T(8,128)S(1)} collective-permute-done((f32[8,128]{1,0:T(8,128)S(1)}, f32[8,128]{1,0:T(8,128)S(1)}, u32[]{:S(2)}, u32[]{:S(2)}) %collective-permute-start.2) | collective-permute-done | bytes 4128 | tf_op jit(solution)/shard_map/ppermute | solution.py:404
  30.9 2.7 %collective-permute-start.3 = (f32[8,128]{1,0:T(8,128)S(1)}, f32[8,128]{1,0:T(8,128)S(1)}, u32[]{:S(2)}, u32[]{:S(2)}) collective-permute-start(f32[8,128]{1,0:T(8,128)S(1)} %add.12), channel_id=1, source_target_pairs={{0,2},{1,3},{2,0},{3,1},{4,6},{5,7},{6,4},{7,5},{8,10},{9,11},{10,... | collective-permute-start | bytes 12296 | tf_op jit(solution)/shard_map/ppermute | solution.py:404
  33.6 1.6 %collective-permute-done.3 = f32[8,128]{1,0:T(8,128)S(1)} collective-permute-done((f32[8,128]{1,0:T(8,128)S(1)}, f32[8,128]{1,0:T(8,128)S(1)}, u32[]{:S(2)}, u32[]{:S(2)}) %collective-permute-start.3) | collective-permute-done | bytes 4128 | tf_op jit(solution)/shard_map/ppermute | solution.py:404
  35.2 1.6 %collective-permute-start.4 = (f32[8,128]{1,0:T(8,128)S(1)}, f32[8,128]{1,0:T(8,128)S(1)}, u32[]{:S(2)}, u32[]{:S(2)}) collective-permute-start(f32[8,128]{1,0:T(8,128)S(1)} %add.13), channel_id=1, source_target_pairs={{0,4},{1,5},{2,6},{3,7},{4,0},{5,1},{6,2},{7,3},{8,12},{9,13},{10,... | collective-permute-start | bytes 12296 | tf_op jit(solution)/shard_map/ppermute | solution.py:404
  36.8 2.0 %collective-permute-done.4 = f32[8,128]{1,0:T(8,128)S(1)} collective-permute-done((f32[8,128]{1,0:T(8,128)S(1)}, f32[8,128]{1,0:T(8,128)S(1)}, u32[]{:S(2)}, u32[]{:S(2)}) %collective-permute-start.4) | collective-permute-done | bytes 4128 | tf_op jit(solution)/shard_map/ppermute | solution.py:404
  38.8 2.6 %collective-permute-start.5 = (f32[8,128]{1,0:T(8,128)S(1)}, f32[8,128]{1,0:T(8,128)S(1)}, u32[]{:S(2)}, u32[]{:S(2)}) collective-permute-start(f32[8,128]{1,0:T(8,128)S(1)} %add.14), channel_id=1, source_target_pairs={{0,8},{1,9},{2,10},{3,11},{4,12},{5,13},{6,14},{7,15},{8,0},{9,1},... | collective-permute-start | bytes 12296 | tf_op jit(solution)/shard_map/ppermute | solution.py:404
  41.4 1.9 %collective-permute-done.5 = f32[8,128]{1,0:T(8,128)S(1)} collective-permute-done((f32[8,128]{1,0:T(8,128)S(1)}, f32[8,128]{1,0:T(8,128)S(1)}, u32[]{:S(2)}, u32[]{:S(2)}) %collective-permute-start.5) | collective-permute-done | bytes 4128 | tf_op jit(solution)/shard_map/ppermute | solution.py:404
  43.4 0.0 copy-start.3
  43.4 0.7 %copy-done.3 = s32[32]{0:T(128)S(1)} copy-done((s32[32]{0:T(128)S(1)}, s32[32]{0:T(128)}, u32[]{:S(2)}) %copy-start.3) | copy-done | bytes 152
  44.0 2.2 %finish.1 = (f32[8,512]{1,0:T(8,128)}, f32[1,32]{1,0:T(1,128)}) custom-call(f32[4,2,17,32,512]{4,3,2,1,0:T(8,128)S(1)} %get-tuple-element.13.refs_0_, f32[1,8,128]{2,1,0:T(8,128)S(1)} %add_bitcast_fusion.refs_1_, f32[17,512]{1,0:T(8,128)S(1)} %get-tuple-element.15.refs_2_, s32[1,32]{1,0:T(1,128)S(1)} %bitcast.6), custom_call_target="tpu_custom_call" | custom-call | tf_op jit(solution)/shard_map/finish/pallas_call | solution.py:407
  (4 shorter events, 0.0 us)
Async XLA Ops:
  0.6 1.2 %copy-start = (f32[32,2,8,512]{3,2,1,0:T(8,128)S(1)}, f32[32,2,8,512]{3,2,1,0:T(8,128)}, u32[]{:S(2)}) copy-start(f32[32,2,8,512]{3,2,1,0:T(8,128)} %param.4) | copy-start | bytes 3145732
  1.9 0.7 %copy-start.1 = (f32[8,512]{1,0:T(8,128)S(1)}, f32[8,512]{1,0:T(8,128)}, u32[]{:S(2)}) copy-start(f32[8,512]{1,0:T(8,128)} %dens.1) | copy-start | bytes 49156
  2.6 0.7 %copy-start.2 = (s32[8,512]{1,0:T(8,128)S(1)}, s32[8,512]{1,0:T(8,128)}, u32[]{:S(2)}) copy-start(s32[8,512]{1,0:T(8,128)} %sup.1) | copy-start | bytes 49156
  4.9 5.9 %collective-permute-start.1 = (f32[330,512]{1,0:T(8,128)S(1)}, f32[330,512]{1,0:T(8,128)S(1)}, u32[]{:S(2)}, u32[]{:S(2)}) collective-permute-start(f32[330,512]{1,0:T(8,128)S(1)} %get-tuple-element.12), channel_id=1, source_target_pairs={{1,0},{2,1},{3,2},{4,3},{5,4},{6,5},{7,6},{8,7},{9,8},{10,9},{11,1... | collective-permute-start | bytes 2027528 | tf_op jit(solution)/shard_map/ppermute | solution.py:376
  6.2 4.6 %collective-permute-start = (f32[264,512]{1,0:T(8,128)S(1)}, f32[264,512]{1,0:T(8,128)S(1)}, u32[]{:S(2)}, u32[]{:S(2)}) collective-permute-start(f32[264,512]{1,0:T(8,128)S(1)} %get-tuple-element.11), channel_id=1, source_target_pairs={{0,1},{1,2},{2,3},{3,4},{4,5},{5,6},{6,7},{7,8},{8,9},{9,10},{10,1... | collective-permute-start | bytes 1622024 | tf_op jit(solution)/shard_map/ppermute | solution.py:375
  16.4 14.6 %collective-permute-start.2 = (f32[8,128]{1,0:T(8,128)S(1)}, f32[8,128]{1,0:T(8,128)S(1)}, u32[]{:S(2)}, u32[]{:S(2)}) collective-permute-start(f32[8,128]{1,0:T(8,128)S(1)} %get-tuple-element.14), channel_id=1, source_target_pairs={{0,1},{1,0},{2,3},{3,2},{4,5},{5,4},{6,7},{7,6},{8,9},{9,8},{10,11... | collective-permute-start | bytes 12296 | tf_op jit(solution)/shard_map/ppermute | solution.py:404
  30.9 4.3 %collective-permute-start.3 = (f32[8,128]{1,0:T(8,128)S(1)}, f32[8,128]{1,0:T(8,128)S(1)}, u32[]{:S(2)}, u32[]{:S(2)}) collective-permute-start(f32[8,128]{1,0:T(8,128)S(1)} %add.12), channel_id=1, source_target_pairs={{0,2},{1,3},{2,0},{3,1},{4,6},{5,7},{6,4},{7,5},{8,10},{9,11},{10,... | collective-permute-start | bytes 12296 | tf_op jit(solution)/shard_map/ppermute | solution.py:404
  35.2 3.6 %collective-permute-start.4 = (f32[8,128]{1,0:T(8,128)S(1)}, f32[8,128]{1,0:T(8,128)S(1)}, u32[]{:S(2)}, u32[]{:S(2)}) collective-permute-start(f32[8,128]{1,0:T(8,128)S(1)} %add.13), channel_id=1, source_target_pairs={{0,4},{1,5},{2,6},{3,7},{4,0},{5,1},{6,2},{7,3},{8,12},{9,13},{10,... | collective-permute-start | bytes 12296 | tf_op jit(solution)/shard_map/ppermute | solution.py:404
  38.8 4.5 %collective-permute-start.5 = (f32[8,128]{1,0:T(8,128)S(1)}, f32[8,128]{1,0:T(8,128)S(1)}, u32[]{:S(2)}, u32[]{:S(2)}) collective-permute-start(f32[8,128]{1,0:T(8,128)S(1)} %add.14), channel_id=1, source_target_pairs={{0,8},{1,9},{2,10},{3,11},{4,12},{5,13},{6,14},{7,15},{8,0},{9,1},... | collective-permute-start | bytes 12296 | tf_op jit(solution)/shard_map/ppermute | solution.py:404
  43.4 0.7 %copy-start.3 = (s32[32]{0:T(128)S(1)}, s32[32]{0:T(128)}, u32[]{:S(2)}) copy-start(s32[32]{0:T(128)} %param.5) | copy-start | bytes 388

commit v2 on v1

--- a/solution.py
+++ b/solution.py
@@ -25,7 +25,7 @@
 
 LANES = 128
 SUB = 8
-CHUNKS = 1
+SHARES = 2
 
 
 def from_next(x, lane):
@@ -68,7 +68,7 @@
     return gx, gy, tw
 
 
-def pack_kernel(part, chunk, pat, dens, sup, own, lo, hi, perm, tmp):
+def pack_kernel(part, base, pat, dens, sup, own, lo, hi, perm, tmp):
     rows, cols = dens.shape
     width = cols // LANES
     j = lax.broadcasted_iota(jnp.int32, (cols, LANES), 0)
@@ -76,7 +76,7 @@
     for c in range(width):
         one = jnp.where(j == width * l + c, 1.0, 0.0).astype(jnp.bfloat16)
         perm[:, c * LANES : (c + 1) * LANES] = one
-    start, size = chunk * part * 2 * rows, part * 2 * rows
+    start, size = base * 2 * rows, part * 2 * rows
     for b in range(0, size, LANES):
         y = rearranged(pat[start + b : start + b + LANES, :], perm[...])
         for c, p in enumerate(pieces(y)):
@@ -95,7 +95,7 @@
                     if r < HI:
                         at = (k * HI + r) * part + g * SUB
                         hi[at : at + SUB, cs] = x
-    if chunk == 0:
+    if base == 0:
         both = jnp.concatenate([dens[...], 1.0 - sup[...].astype(jnp.float32)], 0)
         both = rearranged(both, perm[...])
         for i in range(2):
@@ -108,8 +108,8 @@
             hi[at : at + HI, :] = field[:HI]
 
 
-def krylov_kernel(groups, rows, chunk, own, lo, hi, own0, lo0, hi0, *rest):
-    if chunk:
+def krylov_kernel(groups, rows, base, own, lo, hi, own0, lo0, hi0, *rest):
+    if base:
         before, rest = rest[0], rest[1:]
     v, msg, dext, ea, ec, eh, free, acc = rest
     cols = own.shape[1]
@@ -117,7 +117,8 @@
     lane = lax.broadcasted_iota(jnp.int32, (SUB, LANES), 1)
     sublane = lax.broadcasted_iota(jnp.int32, (SUB, LANES), 0)
     part = groups * SUB
-    lo_base, own_base, hi_base = part * 2 * LO, part * 2 * rows, part * 2 * HI
+    lo_base, own_base = lo0.shape[0] - 2 * LO, own0.shape[0] - 2 * rows
+    hi_base = hi0.shape[0] - 2 * HI
 
     for r in range(total_rows):
         if r < LO:
@@ -212,9 +213,11 @@
         row = jnp.zeros((SUB, LANES), jnp.float32)
         for g in range(groups):
             s = jnp.sum(acc[i, g * SUB : (g + 1) * SUB, :], axis=1, keepdims=True)
-            row = row + jnp.where(lane == sublane + (chunk * part + g * SUB), s, 0.0)
+            row = row + jnp.where(lane == sublane + (base + g * SUB), s, 0.0)
         row = jnp.sum(row, axis=0, keepdims=True)
-        msg[i : i + 1, :] = row + before[i : i + 1, :] if chunk else row
+        row = row + before[0, i : i + 1, :] if base else row
+        for t in range(msg.shape[0]):
+            msg[t, i : i + 1, :] = row
 
 
 def coefficients(m):
@@ -254,8 +257,8 @@
 
 
 def finish_kernel(count, elements, *refs):
-    vs = refs[:CHUNKS]
-    msgs, dext, cases, sens, comp, energy, rimmed, perm = refs[CHUNKS:]
+    vs, refs = refs[:-8], refs[-8:]
+    msgs, dext, cases, sens, comp, energy, rimmed, perm = refs
     rows, cols = sens.shape
     lane = lax.broadcasted_iota(jnp.int32, (SUB, LANES), 1)
     sublane = lax.broadcasted_iota(jnp.int32, (SUB, LANES), 0)
@@ -280,10 +283,11 @@
 
     span = rows + 2
     first = True
+    gi = -1
     for ref in vs:
         groups = ref.shape[3] // SUB
         for g in range(groups):
-            gi = vs.index(ref) * groups + g
+            gi += 1
             at = slice(g * SUB, (g + 1) * SUB)
             co = [by_case(x, gi) for x in xs]
             w = by_case(weight, gi)
@@ -344,8 +348,7 @@
     rows, cols = density.shape
     count = patterns.shape[0]
     tiles = lax.axis_size("space")
-    part = count // CHUNKS
-    groups = part // SUB
+    parts = [count // SHARES] * SHARES
     total_rows = rows + LO + HI
     up = [(i, i + 1) for i in range(tiles - 1)]
     down = [(i + 1, i) for i in range(tiles - 1)]
@@ -357,10 +360,11 @@
         return jax.ShapeDtypeStruct(dims, jnp.float32)
 
     owns, lows, highs = [], [], []
-    for c in range(CHUNKS):
+    for c, part in enumerate(parts):
+        base = sum(parts[:c])
         extra = 0 if c else 2
         own, low, high = pl.pallas_call(
-            functools.partial(pack_kernel, part, c),
+            functools.partial(pack_kernel, part, base),
             out_shape=tuple(shape(n * (2 * part + extra), cols) for n in (rows, LO, HI)),
             in_specs=[vmem] * 3,
             out_specs=(vmem,) * 3,
@@ -376,13 +380,13 @@
         highs.append(lax.ppermute(high, "space", down))
 
     vs, msg = [], None
-    for c in range(CHUNKS):
+    for c, part in enumerate(parts):
         args = (owns[c], lows[c], highs[c], owns[0], lows[0], highs[0]) + ((msg,) if c else ())
         v, msg, dext = pl.pallas_call(
-            functools.partial(krylov_kernel, groups, rows, c),
+            functools.partial(krylov_kernel, part // SUB, rows, sum(parts[:c])),
             out_shape=(
                 shape(ITERS, 2, total_rows, part, cols),
-                shape(MOMENTS, LANES),
+                shape(tiles if c + 1 == len(parts) else 1, MOMENTS, LANES),
                 shape(total_rows, cols),
             ),
             in_specs=[vmem] * len(args),
@@ -395,19 +399,16 @@
                 pltpu.VMEM((MOMENTS, part, LANES), jnp.float32),
             ],
             compiler_params=params,
+            cost_estimate=pl.CostEstimate(flops=10**10, bytes_accessed=40 * 10**6, transcendentals=0),
             name="krylov",
         )(*args)
         vs.append(v)
 
-    b = 1
-    while b < tiles:
-        msg = msg + lax.ppermute(msg, "space", [(i, i ^ b) for i in range(tiles)])
-        b *= 2
-    msgs = msg[None]
+    msgs = lax.all_to_all(msg, "space", 0, 0)
     sens, comp = pl.pallas_call(
         functools.partial(finish_kernel, count, rows * tiles * cols),
         out_shape=(shape(rows, cols), shape(1, count)),
-        in_specs=[vmem] * (CHUNKS + 3),
+        in_specs=[vmem] * (len(vs) + 3),
         out_specs=(vmem,) * 2,
         scratch_shapes=[
             pltpu.VMEM((rows + 2, SUB, cols), jnp.float32),

time: 46.6 us -> 41.9 us (0.90)
  blocking collectives: 0 us -> 17.6 us
  starting transfers between devices: 25 us -> 10.1 us
  waiting for transfers between devices: 7.86 us -> 0.01 us
  Pallas kernels: 9.37 us -> 10.4 us
  local copies, waits for them, and re-layouts: 3.31 us -> 2.66 us
    ppermute x4 -> x0, starting transfers between devices: 20.6 us -> none  [local(): msg = msg + lax.ppermute(msg, 'space', [(i, i ^ b) for i in range(tiles)])]
    all_to_all x0 -> x1, blocking collectives: none -> 17.6 us  [local(): msgs = lax.all_to_all(msg, 'space', 0, 0)]
    ppermute x4 -> x0, waiting for transfers between devices: 6.35 us -> none  [local(): msg = msg + lax.ppermute(msg, 'space', [(i, i ^ b) for i in range(tiles)])]
    ppermute x1 -> x2, starting transfers between devices: 3.06 us -> 7.54 us  [local(): lows.append(lax.ppermute(low, 'space', up))]
    ppermute x1 -> x2, waiting for transfers between devices: 1.51 us -> 0.01 us  [local(): lows.append(lax.ppermute(low, 'space', up))]
    ppermute x1 -> x2, starting transfers between devices: 1.29 us -> 2.58 us  [local(): highs.append(lax.ppermute(high, 'space', down))]
    pallas_call x2 -> x4, Pallas kernels: 7.18 us -> 8.16 us  [the longest x2 6.32 us: local(): pl.pallas_call(functools.partial(krylov_kernel, part // SUB, rows, sum(pa...]
    unnamed x8, local copies, waits for them, and re-layouts: 3.31 us -> 2.66 us
  transfers between devices with their start and end apart: 6 -> 4, of which waited for: 5 -> 0; matrix products, arithmetic and copies ran while one was open for 0% -> 0% of each run, Pallas kernels for 0% -> 10%
where the time goes in v2:
time: 41.9 us; the launch traced here: 41.4 us
  blocking collectives  17.6 us (42%)
  Pallas kernels  10.4 us (25%)
  starting transfers between devices  10.1 us (24%)
  local copies, waits for them, and re-layouts  2.66 us (6%)
  between operations  0.71 us (2%)
    all_to_all x1, blocking collectives, local(): msgs = lax.all_to_all(msg, 'space', 0, 0)  17.6 us
    ppermute x2, starting transfers between devices, local(): lows.append(lax.ppermute(low, 'space', up))  7.54 us
    pallas_call x2, Pallas kernels, local(): pl.pallas_call(functools.partial(krylov_kernel, part // SUB, rows, sum(pa...  6.32 us
    unnamed x8, local copies, waits for them, and re-layouts  2.66 us
    ppermute x2, starting transfers between devices, local(): highs.append(lax.ppermute(high, 'space', down))  2.58 us
    pallas_call x1, Pallas kernels, local(): pl.pallas_call(functools.partial(finish_kernel, count, rows * tiles * col...  2.2 us
    pallas_call x2, Pallas kernels, local(): pl.pallas_call(functools.partial(pack_kernel, part, base), out_shape=tupl...  1.84 us
  transfers between devices with their start and end apart: 4, of which 0 were waited for; matrix products, arithmetic and copies ran while one was open for 0% of the time, Pallas kernels for 10%

profile of v2, /device:TPU:0, one launch (start us, length us, event | category | flops | bytes accessed | tf_op | source)
XLA Modules:
  0.0 41.4 jit_solution(7831117334892767499)
XLA Ops:
  0.6 0.0 copy-start
  0.6 1.2 %copy-done = f32[32,2,8,512]{3,2,1,0:T(8,128)S(1)} copy-done((f32[32,2,8,512]{3,2,1,0:T(8,128)S(1)}, f32[32,2,8,512]{3,2,1,0:T(8,128)}, u32[]{:S(2)}) %copy-start) | copy-done | bytes 1048600
  1.9 0.0 copy-start.1
  1.9 0.7 %copy-done.1 = f32[8,512]{1,0:T(8,128)S(1)} copy-done((f32[8,512]{1,0:T(8,128)S(1)}, f32[8,512]{1,0:T(8,128)}, u32[]{:S(2)}) %copy-start.1) | copy-done | bytes 16408
  2.6 0.0 copy-start.2
  2.6 0.7 %copy-done.2 = s32[8,512]{1,0:T(8,128)S(1)} copy-done((s32[8,512]{1,0:T(8,128)S(1)}, s32[8,512]{1,0:T(8,128)}, u32[]{:S(2)}) %copy-start.2) | copy-done | bytes 16408
  3.3 1.0 %pack.2 = (f32[272,512]{1,0:T(8,128)S(1)}, f32[136,512]{1,0:T(8,128)S(1)}, f32[170,512]{1,0:T(8,128)S(1)}) custom-call(f32[512,512]{1,0:T(8,128)S(1)} %bitcast.3, f32[8,512]{1,0:T(8,128)S(1)} %copy-done.1, s32[8,512]{1,0:T(8,128)S(1)} %copy-done.2), custom_call_target="tpu_custom_call" | custom-call | tf_op jit(solution)/shard_map/pack/pallas_call | solution.py:366
  4.3 1.3 %collective-permute-start.1 = (f32[170,512]{1,0:T(8,128)S(1)}, f32[170,512]{1,0:T(8,128)S(1)}, u32[]{:S(2)}, u32[]{:S(2)}) collective-permute-start(f32[170,512]{1,0:T(8,128)S(1)} %get-tuple-element.17), channel_id=1, source_target_pairs={{1,0},{2,1},{3,2},{4,3},{5,4},{6,5},{7,6},{8,7},{9,8},{10,9},{11,1... | collective-permute-start | bytes 1044488 | tf_op jit(solution)/shard_map/ppermute | solution.py:380
  5.6 3.0 %collective-permute-start = (f32[136,512]{1,0:T(8,128)S(1)}, f32[136,512]{1,0:T(8,128)S(1)}, u32[]{:S(2)}, u32[]{:S(2)}) collective-permute-start(f32[136,512]{1,0:T(8,128)S(1)} %get-tuple-element.16), channel_id=1, source_target_pairs={{0,1},{1,2},{2,3},{3,4},{4,5},{5,6},{6,7},{7,8},{8,9},{9,10},{10,1... | collective-permute-start | bytes 835592 | tf_op jit(solution)/shard_map/ppermute | solution.py:379
  8.6 0.8 %pack.3 = (f32[256,512]{1,0:T(8,128)S(1)}, f32[128,512]{1,0:T(8,128)S(1)}, f32[160,512]{1,0:T(8,128)S(1)}) custom-call(f32[512,512]{1,0:T(8,128)S(1)} %bitcast.4, f32[8,512]{1,0:T(8,128)S(1)} %copy-done.1, s32[8,512]{1,0:T(8,128)S(1)} %copy-done.2), custom_call_target="tpu_custom_call" | custom-call | tf_op jit(solution)/shard_map/pack/pallas_call | solution.py:366
  9.5 4.5 %collective-permute-start.2 = (f32[128,512]{1,0:T(8,128)S(1)}, f32[128,512]{1,0:T(8,128)S(1)}, u32[]{:S(2)}, u32[]{:S(2)}) collective-permute-start(f32[128,512]{1,0:T(8,128)S(1)} %get-tuple-element.20), channel_id=1, source_target_pairs={{0,1},{1,2},{2,3},{3,4},{4,5},{5,6},{6,7},{7,8},{8,9},{9,10},{10,1... | collective-permute-start | bytes 786440 | tf_op jit(solution)/shard_map/ppermute | solution.py:379
  14.0 1.3 %collective-permute-start.3 = (f32[160,512]{1,0:T(8,128)S(1)}, f32[160,512]{1,0:T(8,128)S(1)}, u32[]{:S(2)}, u32[]{:S(2)}) collective-permute-start(f32[160,512]{1,0:T(8,128)S(1)} %get-tuple-element.21), channel_id=1, source_target_pairs={{1,0},{2,1},{3,2},{4,3},{5,4},{6,5},{7,6},{8,7},{9,8},{10,9},{11,1... | collective-permute-start | bytes 983048 | tf_op jit(solution)/shard_map/ppermute | solution.py:380
  15.3 0.0 collective-permute-done.lo.lo0
  15.3 0.0 collective-permute-done.1.hi.hi0
  15.3 3.4 %krylov.2 = (f32[4,2,17,16,512]{4,3,2,1,0:T(8,128)S(1)}, f32[1,8,128]{2,1,0:T(8,128)S(1)}, f32[17,512]{1,0:T(8,128)}) custom-call(f32[272,512]{1,0:T(8,128)S(1)} %get-tuple-element.15.own.own0, f32[136,512]{1,0:T(8,128)S(1)} %collective-permute-done.lo.lo0, f32[170,512]{1,0:T(8,128)S(1)} %collective-permute-done.1.hi.hi0, ...), custom_call_target="tpu_custom_call" | custom-call | flops 10000000000 | bytes 40000000 | tf_op jit(solution)/shard_map/krylov/pallas_call | solution.py:385
  18.7 0.0 collective-permute-done.2.lo
  18.7 0.0 collective-permute-done.3.hi
  18.7 0.0 copy-start.3
  18.7 2.9 %krylov.3 = (f32[4,2,17,16,512]{4,3,2,1,0:T(8,128)S(1)}, f32[16,8,128]{2,1,0:T(8,128)S(1)}, f32[17,512]{1,0:T(8,128)S(1)}) custom-call(f32[256,512]{1,0:T(8,128)S(1)} %get-tuple-element.19.own, f32[128,512]{1,0:T(8,128)S(1)} %collective-permute-done.2.lo, f32[160,512]{1,0:T(8,128)S(1)} %collective-permute-done.3.hi, ...), custom_call_target="tpu_custom_call" | custom-call | flops 10000000000 | bytes 40000000 | tf_op jit(solution)/shard_map/krylov/pallas_call | solution.py:385
  21.7 17.6 %all_to_all.5.refs_2_ = f32[16,8,128]{2,1,0:T(8,128)S(1)} all-to-all(f32[16,8,128]{2,1,0:T(8,128)S(1)} %get-tuple-element.24), channel_id=1, replica_groups=mesh['groups'=2,'space'=16] {'space'}, dimensions={0} | all-to-all | bytes 131072 | tf_op jit(solution)/shard_map/all_to_all | solution.py:407
  39.2 0.0 copy-done.3
  39.2 2.2 %finish.1 = (f32[8,512]{1,0:T(8,128)}, f32[1,32]{1,0:T(1,128)}) custom-call(f32[4,2,17,16,512]{4,3,2,1,0:T(8,128)S(1)} %get-tuple-element.18.refs_0_, f32[4,2,17,16,512]{4,3,2,1,0:T(8,128)S(1)} %get-tuple-element.23.refs_1_, f32[16,8,128]{2,1,0:T(8,128)S(1)} %all_to_all.5.refs_2_, f32[17,512]{1,0:T(8,128)S(1)} %get-tuple-element.25.refs_3_, s32[1,32]{1,0:T(1,128)S(1)} %bitcast.5), custom_call_target="tpu_custom_call" | custom-call | tf_op jit(solution)/shard_map/finish/pallas_call | solution.py:408
Async XLA Ops:
  0.6 1.2 %copy-start = (f32[32,2,8,512]{3,2,1,0:T(8,128)S(1)}, f32[32,2,8,512]{3,2,1,0:T(8,128)}, u32[]{:S(2)}) copy-start(f32[32,2,8,512]{3,2,1,0:T(8,128)} %param.4) | copy-start | bytes 3145732
  1.9 0.7 %copy-start.1 = (f32[8,512]{1,0:T(8,128)S(1)}, f32[8,512]{1,0:T(8,128)}, u32[]{:S(2)}) copy-start(f32[8,512]{1,0:T(8,128)} %dens.3) | copy-start | bytes 49156
  2.6 0.7 %copy-start.2 = (s32[8,512]{1,0:T(8,128)S(1)}, s32[8,512]{1,0:T(8,128)}, u32[]{:S(2)}) copy-start(s32[8,512]{1,0:T(8,128)} %sup.3) | copy-start | bytes 49156
  4.3 11.0 %collective-permute-start.1 = (f32[170,512]{1,0:T(8,128)S(1)}, f32[170,512]{1,0:T(8,128)S(1)}, u32[]{:S(2)}, u32[]{:S(2)}) collective-permute-start(f32[170,512]{1,0:T(8,128)S(1)} %get-tuple-element.17), channel_id=1, source_target_pairs={{1,0},{2,1},{3,2},{4,3},{5,4},{6,5},{7,6},{8,7},{9,8},{10,9},{11,1... | collective-permute-start | bytes 1044488 | tf_op jit(solution)/shard_map/ppermute | solution.py:380
  5.6 9.7 %collective-permute-start = (f32[136,512]{1,0:T(8,128)S(1)}, f32[136,512]{1,0:T(8,128)S(1)}, u32[]{:S(2)}, u32[]{:S(2)}) collective-permute-start(f32[136,512]{1,0:T(8,128)S(1)} %get-tuple-element.16), channel_id=1, source_target_pairs={{0,1},{1,2},{2,3},{3,4},{4,5},{5,6},{6,7},{7,8},{8,9},{9,10},{10,1... | collective-permute-start | bytes 835592 | tf_op jit(solution)/shard_map/ppermute | solution.py:379
  9.5 9.2 %collective-permute-start.2 = (f32[128,512]{1,0:T(8,128)S(1)}, f32[128,512]{1,0:T(8,128)S(1)}, u32[]{:S(2)}, u32[]{:S(2)}) collective-permute-start(f32[128,512]{1,0:T(8,128)S(1)} %get-tuple-element.20), channel_id=1, source_target_pairs={{0,1},{1,2},{2,3},{3,4},{4,5},{5,6},{6,7},{7,8},{8,9},{9,10},{10,1... | collective-permute-start | bytes 786440 | tf_op jit(solution)/shard_map/ppermute | solution.py:379
  14.0 4.7 %collective-permute-start.3 = (f32[160,512]{1,0:T(8,128)S(1)}, f32[160,512]{1,0:T(8,128)S(1)}, u32[]{:S(2)}, u32[]{:S(2)}) collective-permute-start(f32[160,512]{1,0:T(8,128)S(1)} %get-tuple-element.21), channel_id=1, source_target_pairs={{1,0},{2,1},{3,2},{4,3},{5,4},{6,5},{7,6},{8,7},{9,8},{10,9},{11,1... | collective-permute-start | bytes 983048 | tf_op jit(solution)/shard_map/ppermute | solution.py:380
  18.7 20.5 %copy-start.3 = (s32[32]{0:T(128)S(1)}, s32[32]{0:T(128)}, u32[]{:S(2)}) copy-start(s32[32]{0:T(128)} %param.5) | copy-start | bytes 388

commit v3 on v2

--- a/solution.py
+++ b/solution.py
@@ -38,6 +38,14 @@
     return [jnp.where(lane == 0, 0.0, r)] + x[:-1]
 
 
+def taps(lane, up, mid, dn):
+    side = mapped(lambda a, b: a + b, up, dn)
+    total = mapped(lambda a, b: CENTRE * a + EDGE * b, mid, side)
+    sides = mapped(lambda a, b: EDGE * a + CORNER * b, mid, side)
+    left, right = from_prev(sides, lane), from_next(sides, lane)
+    return mapped(lambda a, b, c: a + b + c, total, left, right)
+
+
 def rearranged(x, perm):
     high = x.astype(jnp.bfloat16)
     rest = x - high.astype(jnp.float32)
@@ -68,8 +76,8 @@
     return gx, gy, tw
 
 
-def pack_kernel(part, base, pat, dens, sup, own, lo, hi, perm, tmp):
-    rows, cols = dens.shape
+def pack_kernel(part, base, pat, both, own, lo, hi, perm, tmp):
+    rows, cols = both.shape[0] // 2, both.shape[1]
     width = cols // LANES
     j = lax.broadcasted_iota(jnp.int32, (cols, LANES), 0)
     l = lax.broadcasted_iota(jnp.int32, (cols, LANES), 1)
@@ -96,10 +104,9 @@
                         at = (k * HI + r) * part + g * SUB
                         hi[at : at + SUB, cs] = x
     if base == 0:
-        both = jnp.concatenate([dens[...], 1.0 - sup[...].astype(jnp.float32)], 0)
-        both = rearranged(both, perm[...])
+        mixed = rearranged(both[...], perm[...])
         for i in range(2):
-            field = both[i * rows : (i + 1) * rows]
+            field = mixed[i * rows : (i + 1) * rows]
             at = part * 2 * rows + i * rows
             own[at : at + rows, :] = field
             at = part * 2 * LO + i * LO
@@ -108,10 +115,12 @@
             hi[at : at + HI, :] = field[:HI]
 
 
-def krylov_kernel(groups, rows, base, own, lo, hi, own0, lo0, hi0, *rest):
+def krylov_kernel(groups, rows, base, count, own, lo, hi, own0, lo0, hi0, *rest):
     if base:
         before, rest = rest[0], rest[1:]
-    v, msg, dext, ea, ec, eh, free, acc = rest
+    else:
+        dext, back, divisor, rest = *rest[2:5], rest[:2] + rest[5:]
+    v, msg, ea, ec, eh, free, acc = rest
     cols = own.shape[1]
     total_rows = rows + LO + HI
     lane = lax.broadcasted_iota(jnp.int32, (SUB, LANES), 1)
@@ -133,7 +142,8 @@
             d = hi0[hi_base + k : hi_base + k + 1, :]
             f = hi0[hi_base + HI + k : hi_base + HI + k + 1, :]
         free[r] = jnp.broadcast_to(f, (SUB, cols))
-        dext[r : r + 1, :] = d
+        if not base:
+            dext[r : r + 1, :] = d
         if r < total_rows - 1:
             y = jnp.where(d > 0.0, EMIN + d * d * d * (1.0 - EMIN), 0.0)
             y = jnp.broadcast_to(y, (SUB, cols))
@@ -209,15 +219,44 @@
 
     lax.fori_loop(0, groups, group, 0)
 
-    for i in range(MOMENTS):
+    if not base:
+        i = lax.broadcasted_iota(jnp.int32, (LANES, cols), 0)
+        j = lax.broadcasted_iota(jnp.int32, (LANES, cols), 1)
+        for c in range(cols // LANES):
+            one = jnp.where(j == (cols // LANES) * i + c, 1.0, 0.0).astype(jnp.bfloat16)
+            back[c * LANES : (c + 1) * LANES, :] = one
+        inside = [
+            pieces(jnp.where(dext[LO - 1 + i : LO - 1 + i + rows, :] > 0.0, 1.0, 0.0))
+            for i in range(3)
+        ]
+        ones = taps(lane, *inside)
+        own_d = pieces(dext[LO : LO + rows, :])
+        divisor[...] = jnp.concatenate(mapped(lambda a, b: a * b, ones, own_d), 1)
+
+    per = LANES // count
+    for r in range(msg.shape[1]):
         row = jnp.zeros((SUB, LANES), jnp.float32)
-        for g in range(groups):
-            s = jnp.sum(acc[i, g * SUB : (g + 1) * SUB, :], axis=1, keepdims=True)
-            row = row + jnp.where(lane == sublane + (base + g * SUB), s, 0.0)
+        for i in range(r * per, (r + 1) * per):
+            for g in range(groups):
+                s = jnp.sum(acc[i, g * SUB : (g + 1) * SUB, :], axis=1, keepdims=True)
+                first = (i - r * per) * count + base + g * SUB
+                row = row + jnp.where(lane == sublane + first, s, 0.0)
         row = jnp.sum(row, axis=0, keepdims=True)
-        row = row + before[0, i : i + 1, :] if base else row
+        row = row + before[0, r : r + 1, :] if base else row
         for t in range(msg.shape[0]):
-            msg[t, i : i + 1, :] = row
+            msg[t, r : r + 1, :] = row
+
+
+def exact_sum(terms):
+    pairs = [(t, jnp.zeros_like(t)) for t in terms]
+    while len(pairs) > 1:
+        merged = []
+        for (a, e), (b, f) in zip(pairs[::2], pairs[1::2]):
+            s = a + b
+            v = s - a
+            merged.append((s, ((a - (s - v)) + (b - v)) + (e + f)))
+        pairs = merged + pairs[len(pairs) - len(pairs) % 2 :]
+    return pairs[0][0] + pairs[0][1]
 
 
 def coefficients(m):
@@ -257,22 +296,26 @@
 
 
 def finish_kernel(count, elements, *refs):
-    vs, refs = refs[:-8], refs[-8:]
-    msgs, dext, cases, sens, comp, energy, rimmed, perm = refs
+    vs, refs = refs[:-9], refs[-9:]
+    msgs, dext, back, divisor, cases, sens, comp, energy, rimmed = refs
     rows, cols = sens.shape
     lane = lax.broadcasted_iota(jnp.int32, (SUB, LANES), 1)
     sublane = lax.broadcasted_iota(jnp.int32, (SUB, LANES), 0)
-    m = msgs[0]
-    for i in range(1, msgs.shape[0]):
-        m = m + msgs[i]
-    xs, total = coefficients([m[i : i + 1, :] for i in range(MOMENTS)])
-    real = lax.broadcasted_iota(jnp.int32, (1, LANES), 1) < count
+    m = exact_sum([msgs[i] for i in range(msgs.shape[0])])
+    per = LANES // count
+    moments = []
+    for i in range(MOMENTS):
+        row = jnp.broadcast_to(m[i // per : i // per + 1, :], (SUB, LANES))
+        shift = i % per * count
+        moments.append(pltpu.roll(row, LANES - shift, 1) if shift else row)
+    xs, total = coefficients(moments)
+    real = lane < count
     total = jnp.where(real, total, 0.0)
     mean = jnp.sum(total, axis=1, keepdims=True) / count
     weight = 1.0 / count + 2.0 * KAPPA / count * (total - mean) / mean
 
     def by_case(row, g):
-        s = jnp.where(lane == sublane + g * SUB, jnp.broadcast_to(row, (SUB, LANES)), 0.0)
+        s = jnp.where(lane == sublane + g * SUB, row, 0.0)
         return jnp.broadcast_to(jnp.sum(s, axis=1, keepdims=True), (SUB, LANES))
 
     picked = jnp.zeros((SUB, count), jnp.float32)
@@ -318,30 +361,11 @@
     for e in range(span):
         d = dext[LO - 1 + e : LO + e, :]
         s = jnp.sum(energy[e], axis=0, keepdims=True)
-        rimmed[e : e + 1, :] = (-(elements / mean[:, :1]) * 3.0 * (1.0 - EMIN)) * (d * d * d * s)
-
-    def taps(get):
-        up, mid, dn = get(0), get(1), get(2)
-        side = mapped(lambda a, b: a + b, up, dn)
-        total = mapped(lambda a, b: CENTRE * a + EDGE * b, mid, side)
-        sides = mapped(lambda a, b: EDGE * a + CORNER * b, mid, side)
-        left, right = from_prev(sides, lane), from_next(sides, lane)
-        return mapped(lambda a, b, c: a + b + c, total, left, right)
-
-    width = cols // LANES
-    i = lax.broadcasted_iota(jnp.int32, (LANES, cols), 0)
-    j = lax.broadcasted_iota(jnp.int32, (LANES, cols), 1)
-    for c in range(width):
-        one = jnp.where(j == width * i + c, 1.0, 0.0).astype(jnp.bfloat16)
-        perm[c * LANES : (c + 1) * LANES, :] = one
-
-    top = taps(lambda i: pieces(rimmed[i : i + rows, :]))
-    one = taps(
-        lambda i: pieces(jnp.where(dext[LO - 1 + i : LO - 1 + i + rows, :] > 0.0, 1.0, 0.0))
-    )
-    own = pieces(dext[LO : LO + rows, :])
-    out = jnp.concatenate([t / (o * d) for t, o, d in zip(top, one, own)], 1)
-    sens[...] = rearranged(out, perm[...])
+        rimmed[e : e + 1, :] = (-(elements / mean[:1]) * 3.0 * (1.0 - EMIN)) * (d * d * d * s)
+
+    top = taps(lane, *[pieces(rimmed[i : i + rows, :]) for i in range(3)])
+    out = jnp.concatenate(mapped(lambda a, b: a / b, top, pieces(divisor[...])), 1)
+    sens[...] = rearranged(out, back[...])
 
 
 def local(patterns, cases, density, supports):
@@ -359,6 +383,8 @@
     def shape(*dims):
         return jax.ShapeDtypeStruct(dims, jnp.float32)
 
+    fixed = jnp.pad(supports, ((rows, 0), (0, 0)), constant_values=1)
+    both = jnp.pad(density, ((0, rows), (0, 0))) + (1 - fixed).astype(jnp.float32)
     owns, lows, highs = [], [], []
     for c, part in enumerate(parts):
         base = sum(parts[:c])
@@ -366,7 +392,7 @@
         own, low, high = pl.pallas_call(
             functools.partial(pack_kernel, part, base),
             out_shape=tuple(shape(n * (2 * part + extra), cols) for n in (rows, LO, HI)),
-            in_specs=[vmem] * 3,
+            in_specs=[vmem] * 2,
             out_specs=(vmem,) * 3,
             scratch_shapes=[
                 pltpu.VMEM((cols, cols), jnp.bfloat16),
@@ -374,23 +400,29 @@
             ],
             compiler_params=params,
             name="pack",
-        )(flat, density, supports)
+        )(flat, both)
         owns.append(own)
         lows.append(lax.ppermute(low, "space", up))
         highs.append(lax.ppermute(high, "space", down))
 
-    vs, msg = [], None
+    vs, msg, extras = [], None, None
     for c, part in enumerate(parts):
         args = (owns[c], lows[c], highs[c], owns[0], lows[0], highs[0]) + ((msg,) if c else ())
-        v, msg, dext = pl.pallas_call(
-            functools.partial(krylov_kernel, part // SUB, rows, sum(parts[:c])),
-            out_shape=(
-                shape(ITERS, 2, total_rows, part, cols),
-                shape(tiles if c + 1 == len(parts) else 1, MOMENTS, LANES),
+        outs = (
+            shape(ITERS, 2, total_rows, part, cols),
+            shape(tiles if c + 1 == len(parts) else 1, MOMENTS * count // LANES, LANES),
+        )
+        if not c:
+            outs += (
                 shape(total_rows, cols),
-            ),
+                jax.ShapeDtypeStruct((cols, cols), jnp.bfloat16),
+                shape(rows, cols),
+            )
+        v, msg, *more = pl.pallas_call(
+            functools.partial(krylov_kernel, part // SUB, rows, sum(parts[:c]), count),
+            out_shape=outs,
             in_specs=[vmem] * len(args),
-            out_specs=(vmem,) * 3,
+            out_specs=(vmem,) * len(outs),
             scratch_shapes=[
                 pltpu.VMEM((total_rows - 1, SUB, cols), jnp.float32),
                 pltpu.VMEM((total_rows - 1, SUB, cols), jnp.float32),
@@ -403,21 +435,21 @@
             name="krylov",
         )(*args)
         vs.append(v)
+        extras = extras if c else more
 
     msgs = lax.all_to_all(msg, "space", 0, 0)
     sens, comp = pl.pallas_call(
         functools.partial(finish_kernel, count, rows * tiles * cols),
         out_shape=(shape(rows, cols), shape(1, count)),
-        in_specs=[vmem] * (len(vs) + 3),
+        in_specs=[vmem] * (len(vs) + 5),
         out_specs=(vmem,) * 2,
         scratch_shapes=[
             pltpu.VMEM((rows + 2, SUB, cols), jnp.float32),
             pltpu.VMEM((rows + SUB, cols), jnp.float32),
-            pltpu.VMEM((cols, cols), jnp.bfloat16),
         ],
         compiler_params=params,
         name="finish",
-    )(*vs, msgs, dext, cases[None])
+    )(*vs, msgs, *extras, cases[None])
     return sens, comp.reshape(count)
 
 

time: 41.9 us -> 40.8 us (0.974)
  local copies, waits for them, and re-layouts: 2.66 us -> 1.23 us
  other arithmetic: 0 us -> 0.74 us
  Pallas kernels: 10.4 us -> 9.93 us
    unnamed x8 -> x4, local copies, waits for them, and re-layouts: 2.66 us -> 1.23 us
    add x0 -> x1, other arithmetic: none -> 0.74 us  [local(): jnp.pad(density, ((0, rows), (0, 0))) + (1 - fixed).astype(jnp.float32)]
    pallas_call x2, Pallas kernels: 6.32 us -> 5.87 us  [local(): pl.pallas_call(functools.partial(krylov_kernel, part // SUB, rows, sum(pa...]
  transfers between devices with their start and end apart: 4 -> 4, of which waited for: 0 -> 0; matrix products, arithmetic and copies ran while one was open for 0% -> 0% of each run, Pallas kernels for 10% -> 9%
where the time goes in v3:
time: 40.8 us; the launch traced here: 40.3 us
  blocking collectives  17.6 us (43%)
  starting transfers between devices  10.1 us (25%)
  Pallas kernels  9.93 us (24%)
  local copies, waits for them, and re-layouts  1.23 us (3%)
  other arithmetic  0.74 us (2%)
  between operations  0.73 us (2%)
    all_to_all x1, blocking collectives, local(): msgs = lax.all_to_all(msg, 'space', 0, 0)  17.6 us
    ppermute x2, starting transfers between devices, local(): lows.append(lax.ppermute(low, 'space', up))  7.54 us
    pallas_call x2, Pallas kernels, local(): pl.pallas_call(functools.partial(krylov_kernel, part // SUB, rows, sum(pa...  5.87 us
    ppermute x2, starting transfers between devices, local(): highs.append(lax.ppermute(high, 'space', down))  2.58 us
    pallas_call x1, Pallas kernels, local(): pl.pallas_call(functools.partial(finish_kernel, count, rows * tiles * col...  2.22 us
    pallas_call x2, Pallas kernels, local(): pl.pallas_call(functools.partial(pack_kernel, part, base), out_shape=tupl...  1.84 us
    unnamed x4, local copies, waits for them, and re-layouts  1.23 us
  transfers between devices with their start and end apart: 4, of which 0 were waited for; matrix products, arithmetic and copies ran while one was open for 0% of the time, Pallas kernels for 9%

profile of v3, /device:TPU:0, one launch (start us, length us, event | category | flops | bytes accessed | tf_op | source)
XLA Modules:
  0.0 40.3 jit_solution(4741679271264760220)
XLA Ops:
  0.6 0.7 %convert_add_fusion.both = f32[16,512]{1,0:T(8,128)S(1)} fusion(s32[8,512]{1,0:T(8,128)} %param.7, f32[8,512]{1,0:T(8,128)} %param.6), kind=kLoop, calls=%fused_computation | loop fusion | flops 24576 | bytes 65536 | tf_op jit(solution)/shard_map/add | solution.py:387
  1.4 0.0 copy-start
  1.4 1.2 %copy-done = f32[32,2,8,512]{3,2,1,0:T(8,128)S(1)} copy-done((f32[32,2,8,512]{3,2,1,0:T(8,128)S(1)}, f32[32,2,8,512]{3,2,1,0:T(8,128)}, u32[]{:S(2)}) %copy-start) | copy-done | bytes 1048600
  2.6 1.0 %pack.2 = (f32[272,512]{1,0:T(8,128)S(1)}, f32[136,512]{1,0:T(8,128)S(1)}, f32[170,512]{1,0:T(8,128)S(1)}) custom-call(f32[512,512]{1,0:T(8,128)S(1)} %bitcast.3, f32[16,512]{1,0:T(8,128)S(1)} %convert_add_fusion.both), custom_call_target="tpu_custom_call" | custom-call | tf_op jit(solution)/shard_map/pack/pallas_call | solution.py:392
  3.6 1.3 %collective-permute-start.1 = (f32[170,512]{1,0:T(8,128)S(1)}, f32[170,512]{1,0:T(8,128)S(1)}, u32[]{:S(2)}, u32[]{:S(2)}) collective-permute-start(f32[170,512]{1,0:T(8,128)S(1)} %get-tuple-element.19), channel_id=1, source_target_pairs={{1,0},{2,1},{3,2},{4,3},{5,4},{6,5},{7,6},{8,7},{9,8},{10,9},{11,1... | collective-permute-start | bytes 1044488 | tf_op jit(solution)/shard_map/ppermute | solution.py:406
  4.9 3.0 %collective-permute-start = (f32[136,512]{1,0:T(8,128)S(1)}, f32[136,512]{1,0:T(8,128)S(1)}, u32[]{:S(2)}, u32[]{:S(2)}) collective-permute-start(f32[136,512]{1,0:T(8,128)S(1)} %get-tuple-element.18), channel_id=1, source_target_pairs={{0,1},{1,2},{2,3},{3,4},{4,5},{5,6},{6,7},{7,8},{8,9},{9,10},{10,1... | collective-permute-start | bytes 835592 | tf_op jit(solution)/shard_map/ppermute | solution.py:405
  7.9 0.8 %pack.3 = (f32[256,512]{1,0:T(8,128)S(1)}, f32[128,512]{1,0:T(8,128)S(1)}, f32[160,512]{1,0:T(8,128)S(1)}) custom-call(f32[512,512]{1,0:T(8,128)S(1)} %bitcast.4, f32[16,512]{1,0:T(8,128)S(1)} %convert_add_fusion.both), custom_call_target="tpu_custom_call" | custom-call | tf_op jit(solution)/shard_map/pack/pallas_call | solution.py:392
  8.8 4.5 %collective-permute-start.2 = (f32[128,512]{1,0:T(8,128)S(1)}, f32[128,512]{1,0:T(8,128)S(1)}, u32[]{:S(2)}, u32[]{:S(2)}) collective-permute-start(f32[128,512]{1,0:T(8,128)S(1)} %get-tuple-element.22), channel_id=1, source_target_pairs={{0,1},{1,2},{2,3},{3,4},{4,5},{5,6},{6,7},{7,8},{8,9},{9,10},{10,1... | collective-permute-start | bytes 786440 | tf_op jit(solution)/shard_map/ppermute | solution.py:405
  13.3 1.3 %collective-permute-start.3 = (f32[160,512]{1,0:T(8,128)S(1)}, f32[160,512]{1,0:T(8,128)S(1)}, u32[]{:S(2)}, u32[]{:S(2)}) collective-permute-start(f32[160,512]{1,0:T(8,128)S(1)} %get-tuple-element.23), channel_id=1, source_target_pairs={{1,0},{2,1},{3,2},{4,3},{5,4},{6,5},{7,6},{8,7},{9,8},{10,9},{11,1... | collective-permute-start | bytes 983048 | tf_op jit(solution)/shard_map/ppermute | solution.py:406
  14.6 0.0 collective-permute-done.lo.lo0
  14.6 0.0 collective-permute-done.1.hi.hi0
  14.6 3.0 %krylov.2 = (f32[4,2,17,16,512]{4,3,2,1,0:T(8,128)S(1)}, f32[1,2,128]{2,1,0:T(2,128)S(1)}, f32[17,512]{1,0:T(8,128)S(1)}, bf16[512,512]{1,0:T(8,128)(2,1)S(1)}, f32[8,512]{1,0:T(8,128)S(1)}) custom-call(f32[272,512]{1,0:T(8,128)S(1)} %get-tuple-element.17.own.own0, f32[136,512]{1,0:T(8,128)S(1)} %collective-permute-done.lo.lo0, ...), custom_call_target="tpu_custom_call" | custom-call | flops 10000000000 | bytes 40000000 | tf_op jit(solution)/shard_map/krylov/pallas_call | solution.py:421
  17.6 0.0 collective-permute-done.2.lo
  17.6 0.0 collective-permute-done.3.hi
  17.6 0.0 copy-start.1
  17.6 2.9 %krylov.3 = (f32[4,2,17,16,512]{4,3,2,1,0:T(8,128)S(1)}, f32[16,2,128]{2,1,0:T(2,128)S(1)}) custom-call(f32[256,512]{1,0:T(8,128)S(1)} %get-tuple-element.21.own, f32[128,512]{1,0:T(8,128)S(1)} %collective-permute-done.2.lo, f32[160,512]{1,0:T(8,128)S(1)} %collective-permute-done.3.hi, f32[272,512]{1,0:T(8,128)S(1)} %get-tuple-element.17.own.own0, ...), custom_call_target="tpu_custom_call" | custom-call | flops 10000000000 | bytes 40000000 | tf_op jit(solution)/shard_map/krylov/pallas_call | solution.py:421
  20.5 17.6 %all_to_all.5.refs_2_ = f32[16,2,128]{2,1,0:T(2,128)S(1)} all-to-all(f32[16,2,128]{2,1,0:T(2,128)S(1)} %get-tuple-element.26), channel_id=1, replica_groups=mesh['groups'=2,'space'=16] {'space'}, dimensions={0} | all-to-all | bytes 32768 | tf_op jit(solution)/shard_map/all_to_all | solution.py:440
  38.1 0.0 copy-done.1
  38.1 2.2 %finish.1 = (f32[8,512]{1,0:T(8,128)}, f32[1,32]{1,0:T(1,128)}) custom-call(f32[4,2,17,16,512]{4,3,2,1,0:T(8,128)S(1)} %get-tuple-element.20.refs_0_, f32[4,2,17,16,512]{4,3,2,1,0:T(8,128)S(1)} %get-tuple-element.25.refs_1_, f32[16,2,128]{2,1,0:T(2,128)S(1)} %all_to_all.5.refs_2_, f32[17,512]{1,0:T(8,128)S(1)} %get-tuple-element.27.refs_3_, ...), custom_call_target="tpu_custom_call" | custom-call | tf_op jit(solution)/shard_map/finish/pallas_call | solution.py:441
Async XLA Ops:
  1.4 1.2 %copy-start = (f32[32,2,8,512]{3,2,1,0:T(8,128)S(1)}, f32[32,2,8,512]{3,2,1,0:T(8,128)}, u32[]{:S(2)}) copy-start(f32[32,2,8,512]{3,2,1,0:T(8,128)} %param.4) | copy-start | bytes 3145732
  3.6 11.0 %collective-permute-start.1 = (f32[170,512]{1,0:T(8,128)S(1)}, f32[170,512]{1,0:T(8,128)S(1)}, u32[]{:S(2)}, u32[]{:S(2)}) collective-permute-start(f32[170,512]{1,0:T(8,128)S(1)} %get-tuple-element.19), channel_id=1, source_target_pairs={{1,0},{2,1},{3,2},{4,3},{5,4},{6,5},{7,6},{8,7},{9,8},{10,9},{11,1... | collective-permute-start | bytes 1044488 | tf_op jit(solution)/shard_map/ppermute | solution.py:406
  4.9 9.7 %collective-permute-start = (f32[136,512]{1,0:T(8,128)S(1)}, f32[136,512]{1,0:T(8,128)S(1)}, u32[]{:S(2)}, u32[]{:S(2)}) collective-permute-start(f32[136,512]{1,0:T(8,128)S(1)} %get-tuple-element.18), channel_id=1, source_target_pairs={{0,1},{1,2},{2,3},{3,4},{4,5},{5,6},{6,7},{7,8},{8,9},{9,10},{10,1... | collective-permute-start | bytes 835592 | tf_op jit(solution)/shard_map/ppermute | solution.py:405
  8.8 8.8 %collective-permute-start.2 = (f32[128,512]{1,0:T(8,128)S(1)}, f32[128,512]{1,0:T(8,128)S(1)}, u32[]{:S(2)}, u32[]{:S(2)}) collective-permute-start(f32[128,512]{1,0:T(8,128)S(1)} %get-tuple-element.22), channel_id=1, source_target_pairs={{0,1},{1,2},{2,3},{3,4},{4,5},{5,6},{6,7},{7,8},{8,9},{9,10},{10,1... | collective-permute-start | bytes 786440 | tf_op jit(solution)/shard_map/ppermute | solution.py:405
  13.3 4.3 %collective-permute-start.3 = (f32[160,512]{1,0:T(8,128)S(1)}, f32[160,512]{1,0:T(8,128)S(1)}, u32[]{:S(2)}, u32[]{:S(2)}) collective-permute-start(f32[160,512]{1,0:T(8,128)S(1)} %get-tuple-element.23), channel_id=1, source_target_pairs={{1,0},{2,1},{3,2},{4,3},{5,4},{6,5},{7,6},{8,7},{9,8},{10,9},{11,1... | collective-permute-start | bytes 983048 | tf_op jit(solution)/shard_map/ppermute | solution.py:406
  17.6 20.5 %copy-start.1 = (s32[32]{0:T(128)S(1)}, s32[32]{0:T(128)}, u32[]{:S(2)}) copy-start(s32[32]{0:T(128)} %param.5) | copy-start | bytes 388

commit v4 on v3

--- a/solution.py
+++ b/solution.py
@@ -115,35 +115,52 @@
             hi[at : at + HI, :] = field[:HI]
 
 
-def krylov_kernel(groups, rows, base, count, own, lo, hi, own0, lo0, hi0, *rest):
-    if base:
-        before, rest = rest[0], rest[1:]
+def sweeps(stage, it, rows):
+    end = rows + LO + HI - 2
+    if it == ITERS - 1:
+        runs = {
+            "all": [(LO, LO + rows - 1)],
+            "inner": [(LO + it, LO + rows - 2 - it)],
+            "outer": [(LO, LO + it - 1), (LO + rows - 1 - it, LO + rows - 1)],
+        }
     else:
-        dext, back, divisor, rest = *rest[2:5], rest[:2] + rest[5:]
-    v, msg, ea, ec, eh, free, acc = rest
-    cols = own.shape[1]
+        runs = {
+            "all": [(it, end - it)],
+            "inner": [(LO + it, LO + rows - 2 - it)],
+            "outer": [(it, LO + it), (LO + rows - 2 - it, end - it)],
+        }
+    return runs[stage]
+
+
+def krylov_kernel(groups, rows, base, count, stage, *refs):
+    if stage == "inner":
+        own, ea, ec, eh, free, v, acc = refs
+    elif stage == "outer":
+        lo, hi, ea, ec, eh, free, before, _, start, v, msg, acc = refs
+    else:
+        own, lo, hi, v, msg, ea, ec, eh, free, dext, back, divisor, acc = refs
+    part = groups * SUB
+    cols = v.shape[-1]
     total_rows = rows + LO + HI
     lane = lax.broadcasted_iota(jnp.int32, (SUB, LANES), 1)
     sublane = lax.broadcasted_iota(jnp.int32, (SUB, LANES), 0)
     part = groups * SUB
-    lo_base, own_base = lo0.shape[0] - 2 * LO, own0.shape[0] - 2 * rows
-    hi_base = hi0.shape[0] - 2 * HI
-
-    for r in range(total_rows):
+    lo_base, own_base, hi_base = part * 2 * LO, part * 2 * rows, part * 2 * HI
+
+    for r in range(total_rows if stage == "all" else 0):
         if r < LO:
-            d = lo0[lo_base + r : lo_base + r + 1, :]
-            f = lo0[lo_base + LO + r : lo_base + LO + r + 1, :]
+            d = lo[lo_base + r : lo_base + r + 1, :]
+            f = lo[lo_base + LO + r : lo_base + LO + r + 1, :]
         elif r < LO + rows:
             k = own_base + r - LO
-            d = own0[k : k + 1, :]
-            f = own0[k + rows : k + rows + 1, :]
+            d = own[k : k + 1, :]
+            f = own[k + rows : k + rows + 1, :]
         else:
             k = r - LO - rows
-            d = hi0[hi_base + k : hi_base + k + 1, :]
-            f = hi0[hi_base + HI + k : hi_base + HI + k + 1, :]
+            d = hi[hi_base + k : hi_base + k + 1, :]
+            f = hi[hi_base + HI + k : hi_base + HI + k + 1, :]
         free[r] = jnp.broadcast_to(f, (SUB, cols))
-        if not base:
-            dext[r : r + 1, :] = d
+        dext[r : r + 1, :] = d
         if r < total_rows - 1:
             y = jnp.where(d > 0.0, EMIN + d * d * d * (1.0 - EMIN), 0.0)
             y = jnp.broadcast_to(y, (SUB, cols))
@@ -154,6 +171,8 @@
     def group(g, _):
         at = pl.ds(pl.multiple_of(g * SUB, SUB), SUB)
         for r in range(total_rows):
+            if stage == ("outer" if LO <= r < LO + rows else "inner"):
+                continue
             for k in range(2):
                 if r < LO:
                     x = lo[pl.ds(pl.multiple_of((k * LO + r) * part + g * SUB, SUB), SUB), :]
@@ -163,7 +182,7 @@
                     x = hi[pl.ds(pl.multiple_of((k * HI + r - LO - rows) * part + g * SUB, SUB), SUB), :]
                 v[0, k, r, at, :] = x * free[r]
 
-        sums = [None] * MOMENTS
+        sums = [start[i, at, :] if stage == "outer" else None for i in range(MOMENTS)]
 
         def add(i, a, b):
             for p, q in zip(a, b):
@@ -171,55 +190,56 @@
 
         for it in range(ITERS):
             last = it == ITERS - 1
-            first_e = LO if last else it
-            last_e = LO + rows - 1 if last else total_rows - 2 - it
-            here = [pair_modes(pieces(v[it, k, first_e, at, :]), lane) for k in range(2)]
-            prior = None
-            for e in range(first_e, last_e + 1):
-                above = [pair_modes(pieces(v[it, k, e + 1, at, :]), lane) for k in range(2)]
-                gxu, gyu, twu = element_modes(here[0], above[0])
-                gxv, gyv, twv = element_modes(here[1], above[1])
-                here = above
-                a, c, h = pieces(ea[e]), pieces(ec[e]), pieces(eh[e])
-                tx = mapped(lambda y, s, t: y * (s + NU * t), a, gxu, gyv)
-                ty = mapped(lambda y, s, t: y * (NU * s + t), a, gxu, gyv)
-                gs = mapped(lambda s, t: s + t, gyu, gxv)
-                tg = mapped(lambda y, s: y * s, c, gs)
-                hu = mapped(lambda y, s: y * s, h, twu)
-                hv = mapped(lambda y, s: y * s, h, twv)
-                if last:
-                    for s, t in ((tx, gxu), (ty, gyv), (tg, gs), (hu, twu), (hv, twv)):
-                        add(MOMENTS - 1, s, t)
-                    continue
-                up = [
-                    (tx, mapped(lambda s, t: s + t, tg, hu)),
-                    (tg, mapped(lambda s, t: s + t, ty, hv)),
-                ]
-                if prior is not None:
-                    dn = [mapped(lambda s, t: s - t, tg, hu), mapped(lambda s, t: s - t, ty, hv)]
-                    mask = pieces(free[e])
-                    for k in range(2):
-                        t = mapped(lambda s, t: s - t, prior[k][0], up[k][0])
-                        q = mapped(lambda s, t: s + t, prior[k][1], dn[k])
-                        left = mapped(lambda s, t: s - t, t, q)
-                        right = from_prev(mapped(lambda s, t: s + t, t, q), lane)
-                        out = mapped(lambda s, t, m: (s + t) * m, left, right, mask)
-                        for c0, o in enumerate(out):
-                            v[it + 1, k, e, at, c0 * LANES : (c0 + 1) * LANES] = o
-                        if LO <= e < LO + rows:
-                            src = pieces(v[it, k, e, at, :])
-                            if it == 0:
-                                add(0, src, src)
-                            add(2 * it + 1, src, out)
-                            add(2 * it + 2, out, out)
-                prior = up
+            for first_e, last_e in sweeps(stage, it, rows):
+                here = [pair_modes(pieces(v[it, k, first_e, at, :]), lane) for k in range(2)]
+                prior = None
+                for e in range(first_e, last_e + 1):
+                    above = [pair_modes(pieces(v[it, k, e + 1, at, :]), lane) for k in range(2)]
+                    gxu, gyu, twu = element_modes(here[0], above[0])
+                    gxv, gyv, twv = element_modes(here[1], above[1])
+                    here = above
+                    a, c, h = pieces(ea[e]), pieces(ec[e]), pieces(eh[e])
+                    tx = mapped(lambda y, s, t: y * (s + NU * t), a, gxu, gyv)
+                    ty = mapped(lambda y, s, t: y * (NU * s + t), a, gxu, gyv)
+                    gs = mapped(lambda s, t: s + t, gyu, gxv)
+                    tg = mapped(lambda y, s: y * s, c, gs)
+                    hu = mapped(lambda y, s: y * s, h, twu)
+                    hv = mapped(lambda y, s: y * s, h, twv)
+                    if last:
+                        for s, t in ((tx, gxu), (ty, gyv), (tg, gs), (hu, twu), (hv, twv)):
+                            add(MOMENTS - 1, s, t)
+                        continue
+                    up = [
+                        (tx, mapped(lambda s, t: s + t, tg, hu)),
+                        (tg, mapped(lambda s, t: s + t, ty, hv)),
+                    ]
+                    if prior is not None:
+                        dn = [mapped(lambda s, t: s - t, tg, hu), mapped(lambda s, t: s - t, ty, hv)]
+                        mask = pieces(free[e])
+                        for k in range(2):
+                            t = mapped(lambda s, t: s - t, prior[k][0], up[k][0])
+                            q = mapped(lambda s, t: s + t, prior[k][1], dn[k])
+                            left = mapped(lambda s, t: s - t, t, q)
+                            right = from_prev(mapped(lambda s, t: s + t, t, q), lane)
+                            out = mapped(lambda s, t, m: (s + t) * m, left, right, mask)
+                            for c0, o in enumerate(out):
+                                v[it + 1, k, e, at, c0 * LANES : (c0 + 1) * LANES] = o
+                            if LO <= e < LO + rows:
+                                src = pieces(v[it, k, e, at, :])
+                                if it == 0:
+                                    add(0, src, src)
+                                add(2 * it + 1, src, out)
+                                add(2 * it + 2, out, out)
+                    prior = up
         for i in range(MOMENTS):
             acc[i, at, :] = sums[i]
         return 0
 
     lax.fori_loop(0, groups, group, 0)
 
-    if not base:
+    if stage == "inner":
+        return
+    if stage == "all":
         i = lax.broadcasted_iota(jnp.int32, (LANES, cols), 0)
         j = lax.broadcasted_iota(jnp.int32, (LANES, cols), 1)
         for c in range(cols // LANES):
@@ -405,37 +425,46 @@
         lows.append(lax.ppermute(low, "space", up))
         highs.append(lax.ppermute(high, "space", down))
 
-    vs, msg, extras = [], None, None
-    for c, part in enumerate(parts):
-        args = (owns[c], lows[c], highs[c], owns[0], lows[0], highs[0]) + ((msg,) if c else ())
-        outs = (
-            shape(ITERS, 2, total_rows, part, cols),
-            shape(tiles if c + 1 == len(parts) else 1, MOMENTS * count // LANES, LANES),
-        )
-        if not c:
-            outs += (
-                shape(total_rows, cols),
-                jax.ShapeDtypeStruct((cols, cols), jnp.bfloat16),
-                shape(rows, cols),
-            )
-        v, msg, *more = pl.pallas_call(
-            functools.partial(krylov_kernel, part // SUB, rows, sum(parts[:c]), count),
+    vs, msg, fields, extras = [], None, (), ()
+    def krylov(c, stage, args, outs, **options):
+        part = parts[c]
+        return pl.pallas_call(
+            functools.partial(krylov_kernel, part // SUB, rows, sum(parts[:c]), count, stage),
             out_shape=outs,
             in_specs=[vmem] * len(args),
             out_specs=(vmem,) * len(outs),
-            scratch_shapes=[
-                pltpu.VMEM((total_rows - 1, SUB, cols), jnp.float32),
-                pltpu.VMEM((total_rows - 1, SUB, cols), jnp.float32),
-                pltpu.VMEM((total_rows - 1, SUB, cols), jnp.float32),
-                pltpu.VMEM((total_rows, SUB, cols), jnp.float32),
-                pltpu.VMEM((MOMENTS, part, LANES), jnp.float32),
-            ],
             compiler_params=params,
-            cost_estimate=pl.CostEstimate(flops=10**10, bytes_accessed=40 * 10**6, transcendentals=0),
+            cost_estimate=pl.CostEstimate(
+                flops=10**10, bytes_accessed=40 * 10**6, transcendentals=0
+            ),
             name="krylov",
+            **options,
         )(*args)
+
+    for c, part in enumerate(parts):
+        vectors = shape(ITERS, 2, total_rows, part, cols)
+        sums = shape(MOMENTS, part, LANES)
+        sends = tiles if c + 1 == len(parts) else 1
+        message = shape(sends, MOMENTS * count // LANES, LANES)
+        scratch = [pltpu.VMEM(sums.shape, jnp.float32)]
+        if c:
+            v, start = krylov(c, "inner", (owns[c], *fields), (vectors, sums))
+            v, msg = krylov(
+                c,
+                "outer",
+                (lows[c], highs[c], *fields, msg, v, start),
+                (vectors, message),
+                scratch_shapes=scratch,
+                input_output_aliases={7: 0},
+            )
+        else:
+            outs = (vectors, message) + (shape(total_rows - 1, SUB, cols),) * 3
+            outs += (shape(total_rows, SUB, cols), shape(total_rows, cols))
+            outs += (jax.ShapeDtypeStruct((cols, cols), jnp.bfloat16), shape(rows, cols))
+            args = (owns[c], lows[c], highs[c])
+            v, msg, *more = krylov(c, "all", args, outs, scratch_shapes=scratch)
+            fields, extras = more[:4], more[4:]
         vs.append(v)
-        extras = extras if c else more
 
     msgs = lax.all_to_all(msg, "space", 0, 0)
     sens, comp = pl.pallas_call(

time: 40.8 us -> 40.1 us (0.983)
  blocking collectives: 17.6 us -> 16.2 us
  Pallas kernels: 9.93 us -> 10.7 us
    all_to_all x1, blocking collectives: 17.6 us -> 16.2 us  [local(): msgs = lax.all_to_all(msg, 'space', 0, 0)]
    pallas_call x2 -> x3, Pallas kernels: 5.87 us -> 6.56 us  [krylov(): pl.pallas_call(functools.partial(krylov_kernel, part // SUB, rows, sum(pa...]
  transfers between devices with their start and end apart: 4 -> 4, of which waited for: 0 -> 0; matrix products, arithmetic and copies ran while one was open for 0% -> 0% of each run, Pallas kernels for 9% -> 13%
where the time goes in v4:
time: 40.1 us; the launch traced here: 39.7 us
  blocking collectives  16.2 us (40%)
  Pallas kernels  10.7 us (27%)
  starting transfers between devices  10.1 us (25%)
  local copies, waits for them, and re-layouts  1.23 us (3%)
  other arithmetic  0.74 us (2%)
  between operations  0.73 us (2%)
    all_to_all x1, blocking collectives, local(): msgs = lax.all_to_all(msg, 'space', 0, 0)  16.2 us
    ppermute x2, starting transfers between devices, local(): lows.append(lax.ppermute(low, 'space', up))  7.54 us
    pallas_call x3, Pallas kernels, krylov(): pl.pallas_call(functools.partial(krylov_kernel, part // SUB, rows, sum(pa...  6.56 us
    ppermute x2, starting transfers between devices, local(): highs.append(lax.ppermute(high, 'space', down))  2.58 us
    pallas_call x1, Pallas kernels, local(): pl.pallas_call(functools.partial(finish_kernel, count, rows * tiles * col...  2.22 us
    pallas_call x2, Pallas kernels, local(): pl.pallas_call(functools.partial(pack_kernel, part, base), out_shape=tupl...  1.9 us
    unnamed x4, local copies, waits for them, and re-layouts  1.23 us
  transfers between devices with their start and end apart: 4, of which 0 were waited for; matrix products, arithmetic and copies ran while one was open for 0% of the time, Pallas kernels for 13%

profile of v4, /device:TPU:0, one launch (start us, length us, event | category | flops | bytes accessed | tf_op | source)
XLA Modules:
  0.0 39.7 jit_solution(7469208004537264862)
XLA Ops:
  0.6 0.7 %convert_add_fusion.both = f32[16,512]{1,0:T(8,128)S(1)} fusion(s32[8,512]{1,0:T(8,128)} %param.7, f32[8,512]{1,0:T(8,128)} %param.6), kind=kLoop, calls=%fused_computation | loop fusion | flops 24576 | bytes 65536 | tf_op jit(solution)/shard_map/add | solution.py:407
  1.4 0.0 copy-start
  1.4 1.2 %copy-done = f32[32,2,8,512]{3,2,1,0:T(8,128)S(1)} copy-done((f32[32,2,8,512]{3,2,1,0:T(8,128)S(1)}, f32[32,2,8,512]{3,2,1,0:T(8,128)}, u32[]{:S(2)}) %copy-start) | copy-done | bytes 1048600
  2.6 1.0 %pack.2 = (f32[272,512]{1,0:T(8,128)S(1)}, f32[136,512]{1,0:T(8,128)S(1)}, f32[170,512]{1,0:T(8,128)S(1)}) custom-call(f32[512,512]{1,0:T(8,128)S(1)} %bitcast.3, f32[16,512]{1,0:T(8,128)S(1)} %convert_add_fusion.both), custom_call_target="tpu_custom_call" | custom-call | tf_op jit(solution)/shard_map/pack/pallas_call | solution.py:412
  3.6 1.3 %collective-permute-start.1 = (f32[170,512]{1,0:T(8,128)S(1)}, f32[170,512]{1,0:T(8,128)S(1)}, u32[]{:S(2)}, u32[]{:S(2)}) collective-permute-start(f32[170,512]{1,0:T(8,128)S(1)} %get-tuple-element.25), channel_id=1, source_target_pairs={{1,0},{2,1},{3,2},{4,3},{5,4},{6,5},{7,6},{8,7},{9,8},{10,9},{11,1... | collective-permute-start | bytes 1044488 | tf_op jit(solution)/shard_map/ppermute | solution.py:426
  4.9 3.0 %collective-permute-start = (f32[136,512]{1,0:T(8,128)S(1)}, f32[136,512]{1,0:T(8,128)S(1)}, u32[]{:S(2)}, u32[]{:S(2)}) collective-permute-start(f32[136,512]{1,0:T(8,128)S(1)} %get-tuple-element.24), channel_id=1, source_target_pairs={{0,1},{1,2},{2,3},{3,4},{4,5},{5,6},{6,7},{7,8},{8,9},{9,10},{10,1... | collective-permute-start | bytes 835592 | tf_op jit(solution)/shard_map/ppermute | solution.py:425
  8.0 0.9 %pack.3 = (f32[256,512]{1,0:T(8,128)S(1)}, f32[128,512]{1,0:T(8,128)S(1)}, f32[160,512]{1,0:T(8,128)S(1)}) custom-call(f32[512,512]{1,0:T(8,128)S(1)} %bitcast.4, f32[16,512]{1,0:T(8,128)S(1)} %convert_add_fusion.both), custom_call_target="tpu_custom_call" | custom-call | tf_op jit(solution)/shard_map/pack/pallas_call | solution.py:412
  8.9 4.5 %collective-permute-start.2 = (f32[128,512]{1,0:T(8,128)S(1)}, f32[128,512]{1,0:T(8,128)S(1)}, u32[]{:S(2)}, u32[]{:S(2)}) collective-permute-start(f32[128,512]{1,0:T(8,128)S(1)} %get-tuple-element.27), channel_id=1, source_target_pairs={{0,1},{1,2},{2,3},{3,4},{4,5},{5,6},{6,7},{7,8},{8,9},{9,10},{10,1... | collective-permute-start | bytes 786440 | tf_op jit(solution)/shard_map/ppermute | solution.py:425
  13.4 1.3 %collective-permute-start.3 = (f32[160,512]{1,0:T(8,128)S(1)}, f32[160,512]{1,0:T(8,128)S(1)}, u32[]{:S(2)}, u32[]{:S(2)}) collective-permute-start(f32[160,512]{1,0:T(8,128)S(1)} %get-tuple-element.28), channel_id=1, source_target_pairs={{1,0},{2,1},{3,2},{4,3},{5,4},{6,5},{7,6},{8,7},{9,8},{10,9},{11,1... | collective-permute-start | bytes 983048 | tf_op jit(solution)/shard_map/ppermute | solution.py:426
  14.7 0.0 collective-permute-done.refs_1_
  14.7 0.0 collective-permute-done.1.refs_2_
  14.7 3.1 %krylov.3 = (f32[4,2,17,16,512]{4,3,2,1,0:T(8,128)S(1)}, f32[1,2,128]{2,1,0:T(2,128)S(1)}, f32[16,8,512]{2,1,0:T(8,128)S(1)}, f32[16,8,512]{2,1,0:T(8,128)S(1)},...) custom-call(f32[272,512]{1,0:T(8,128)S(1)} %get-tuple-element.23.ref, ...), custom_call_target="tpu_custom_call" | custom-call | flops 10000000000 | bytes 40000000 | tf_op jit(solution)/shard_map/krylov/pallas_call | solution.py:431
  17.8 1.3 %krylov.4 = (f32[4,2,17,16,512]{4,3,2,1,0:T(8,128)S(1)}, f32[8,16,128]{2,1,0:T(8,128)S(1)}) custom-call(f32[256,512]{1,0:T(8,128)S(1)} %get-tuple-element.34.refs_0_, f32[16,8,512]{2,1,0:T(8,128)S(1)} %get-tuple-element.29.refs_1_.refs_2_, f32[16,8,512]{2,1,0:T(8,128)S(1)} %get-tuple-element.30.refs_2_.refs_3_, ...), custom_call_target="tpu_custom_call" | custom-call | flops 10000000000 | bytes 40000000 | tf_op jit(solution)/shard_map/krylov/pallas_call | solution.py:431
  19.0 0.0 collective-permute-done.2.refs_0_
  19.1 0.0 collective-permute-done.3.refs_1_
  19.1 0.0 copy-start.1
  19.1 2.2 %krylov.5 = (f32[4,2,17,16,512]{4,3,2,1,0:T(8,128)S(1)}, f32[16,2,128]{2,1,0:T(2,128)S(1)}) custom-call(f32[128,512]{1,0:T(8,128)S(1)} %collective-permute-done.2.refs_0_, f32[160,512]{1,0:T(8,128)S(1)} %collective-permute-done.3.refs_1_, f32[16,8,512]{2,1,0:T(8,128)S(1)} %get-tuple-element.29.refs_1_.refs_2_, ...), custom_call_target="tpu_custom_call", output_to_operand_aliasing={{0}: (7, {})} | custom-call | flops 10000000000 | bytes 40000000 | tf_op jit(solution)/shard_map/krylov/pallas_call | solution.py:431
  21.3 16.2 %all_to_all.5.refs_2_ = f32[16,2,128]{2,1,0:T(2,128)S(1)} all-to-all(f32[16,2,128]{2,1,0:T(2,128)S(1)} %get-tuple-element.38), channel_id=1, replica_groups=mesh['groups'=2,'space'=16] {'space'}, dimensions={0} | all-to-all | bytes 32768 | tf_op jit(solution)/shard_map/all_to_all | solution.py:469
  37.5 0.0 copy-done.1
  37.5 2.2 %finish.1 = (f32[8,512]{1,0:T(8,128)}, f32[1,32]{1,0:T(1,128)}) custom-call(f32[4,2,17,16,512]{4,3,2,1,0:T(8,128)S(1)} %get-tuple-element.26.refs_0_, f32[4,2,17,16,512]{4,3,2,1,0:T(8,128)S(1)} %get-tuple-element.37.refs_1_, f32[16,2,128]{2,1,0:T(2,128)S(1)} %all_to_all.5.refs_2_, f32[17,512]{1,0:T(8,128)S(1)} %get-tuple-element.39.refs_3_, ...), custom_call_target="tpu_custom_call" | custom-call | tf_op jit(solution)/shard_map/finish/pallas_call | solution.py:470
Async XLA Ops:
  1.4 1.2 %copy-start = (f32[32,2,8,512]{3,2,1,0:T(8,128)S(1)}, f32[32,2,8,512]{3,2,1,0:T(8,128)}, u32[]{:S(2)}) copy-start(f32[32,2,8,512]{3,2,1,0:T(8,128)} %param.4) | copy-start | bytes 3145732
  3.6 11.0 %collective-permute-start.1 = (f32[170,512]{1,0:T(8,128)S(1)}, f32[170,512]{1,0:T(8,128)S(1)}, u32[]{:S(2)}, u32[]{:S(2)}) collective-permute-start(f32[170,512]{1,0:T(8,128)S(1)} %get-tuple-element.25), channel_id=1, source_target_pairs={{1,0},{2,1},{3,2},{4,3},{5,4},{6,5},{7,6},{8,7},{9,8},{10,9},{11,1... | collective-permute-start | bytes 1044488 | tf_op jit(solution)/shard_map/ppermute | solution.py:426
  4.9 9.7 %collective-permute-start = (f32[136,512]{1,0:T(8,128)S(1)}, f32[136,512]{1,0:T(8,128)S(1)}, u32[]{:S(2)}, u32[]{:S(2)}) collective-permute-start(f32[136,512]{1,0:T(8,128)S(1)} %get-tuple-element.24), channel_id=1, source_target_pairs={{0,1},{1,2},{2,3},{3,4},{4,5},{5,6},{6,7},{7,8},{8,9},{9,10},{10,1... | collective-permute-start | bytes 835592 | tf_op jit(solution)/shard_map/ppermute | solution.py:425
  8.9 10.2 %collective-permute-start.2 = (f32[128,512]{1,0:T(8,128)S(1)}, f32[128,512]{1,0:T(8,128)S(1)}, u32[]{:S(2)}, u32[]{:S(2)}) collective-permute-start(f32[128,512]{1,0:T(8,128)S(1)} %get-tuple-element.27), channel_id=1, source_target_pairs={{0,1},{1,2},{2,3},{3,4},{4,5},{5,6},{6,7},{7,8},{8,9},{9,10},{10,1... | collective-permute-start | bytes 786440 | tf_op jit(solution)/shard_map/ppermute | solution.py:425
  13.4 5.7 %collective-permute-start.3 = (f32[160,512]{1,0:T(8,128)S(1)}, f32[160,512]{1,0:T(8,128)S(1)}, u32[]{:S(2)}, u32[]{:S(2)}) collective-permute-start(f32[160,512]{1,0:T(8,128)S(1)} %get-tuple-element.28), channel_id=1, source_target_pairs={{1,0},{2,1},{3,2},{4,3},{5,4},{6,5},{7,6},{8,7},{9,8},{10,9},{11,1... | collective-permute-start | bytes 983048 | tf_op jit(solution)/shard_map/ppermute | solution.py:426
  19.1 18.4 %copy-start.1 = (s32[32]{0:T(128)S(1)}, s32[32]{0:T(128)}, u32[]{:S(2)}) copy-start(s32[32]{0:T(128)} %param.5) | copy-start | bytes 388
